TPU v7x, 256 devices: a whole 4x4x8 slice. The times are simulated.
256 devices in a mesh: idx: 64 (over z, y, core), con: 4 (over x).
Axes of the slice: x: 4, y: 4, z: 8, core: 2. Of those that a mesh axis runs over, the one named last changes fastest.
Arguments:
- amplitude: bfloat16 [512, 8, 800], P('idx'), may hold values from -6 to 6
- pair_irrep: int32 [512], replicated, may hold values from 0 to 7
- fit_ac: bfloat16 [1024, 64, 8], P('con'), may hold values from -6 to 6
- fitting_tensor_bd: bfloat16 [1024, 1024, 800], P('con', 'idx'), may hold values from -0.0068359375 to 0.0068359375
- a_irrep: int32 [64], replicated, may hold values from 0 to 7
- c_irrep: int32 [8], replicated, may hold values from 0 to 7
- irrep_start: int32 [8], replicated, may hold values from 0 to 640, as said below
- product: int32 [8, 8], replicated, may hold values from 0 to 7, as said below
- tile_len: int32 [64], replicated, may hold values from 1 to 16, 800 in all
- tile_irrep: int32 [64], replicated, may hold values from 0 to 7
Outputs:
- residual: float32 [512, 64, 1024], P(('idx', 'con'))
Inputs may be any that keep to these rules, and one draw needn't show every extreme that they name: Irrep blocks are contiguous in d, in order of g; each holds at least one orbital and at most 160; the last block holds exactly 160; irrep_start[0] is 0. product is the table of a commutative group in which every element is its own inverse. `tile_len`: the tile lengths sum to 800; some tile is full.
All inputs are finite; a program needn't handle non-finite values.
Results may differ from a plain program's by a relative error of at most 0.0029.
Values may be sent and summed in bfloat16 or wider, within the bound.
A program may use at most 192 MiB of HBM per device.

v0:
```python
import jax
import jax.numpy as jnp
from jax import lax
from jax.sharding import PartitionSpec as P

BW = 16


def irrep_hits(labels, count):
    return (labels[:, None] == jnp.arange(count, dtype=jnp.int32)[None, :]).astype(jnp.int32)


def table_lookup(product, left, right):
    count = product.shape[0]
    return jnp.einsum("px,xy,cy->pc", irrep_hits(left, count), product, irrep_hits(right, count))


def orbital_irreps(irrep_start, width):
    spots = jnp.arange(width, dtype=jnp.int32)
    return jnp.sum((spots[:, None] >= irrep_start[None, :]).astype(jnp.int32), axis=1) - 1


def body(
    amplitude,
    pair_irrep,
    fit_ac,
    fitting_tensor_bd,
    a_irrep,
    c_irrep,
    irrep_start,
    product,
    tile_len,
    tile_irrep,
):
    local_pairs, n_c, n_v = amplitude.shape
    con_count = lax.axis_size("con")
    d_irrep = orbital_irreps(irrep_start, n_v)
    first = lax.axis_index("idx") * local_pairs
    own_irrep = lax.dynamic_slice_in_dim(pair_irrep, first, local_pairs, 0)
    target = table_lookup(product, own_irrep, c_irrep)
    fitted_result = lax.dot_general(
        fit_ac, fitting_tensor_bd, (((0,), (0,)), ((), ())), preferred_element_type=jnp.float32
    ).astype(jnp.bfloat16)
    allowed = d_irrep[None, None, :] == target[:, :, None]
    masked = jnp.where(allowed, amplitude, jnp.zeros_like(amplitude))
    partial_value = jnp.einsum(
        "pcd,acbd->pab",
        lax.all_gather(masked, "idx", axis=0, tiled=True),
        fitted_result,
        preferred_element_type=jnp.float32,
    )
    moved = lax.all_to_all(partial_value, "idx", split_axis=0, concat_axis=2, tiled=True)
    summed = lax.psum_scatter(moved, "con", scatter_dimension=0, tiled=True)
    out_pairs = summed.shape[0]
    width_all = summed.shape[2]
    out_first = (lax.axis_index("idx") * con_count + lax.axis_index("con")) * out_pairs
    out_irrep = lax.dynamic_slice_in_dim(pair_irrep, out_first, out_pairs, 0)
    slot_ids = jnp.arange(width_all, dtype=jnp.int32)
    live = slot_ids % BW < jnp.repeat(tile_len, BW)
    b_irrep = jnp.repeat(tile_irrep, BW)
    pair_ab = table_lookup(product, a_irrep, b_irrep)
    keep = (pair_ab[None, :, :] == out_irrep[:, None, None]) & live[None, None, :]
    return jnp.where(keep, summed, jnp.zeros_like(summed))


def solution(mesh):
    placed = (
        P("idx", None, None),
        P(),
        P("con", None, None),
        P("con", "idx", None),
        P(),
        P(),
        P(),
        P(),
        P(),
        P(),
    )
    return jax.shard_map(
        body, mesh=mesh, in_specs=placed, out_specs=P(("idx", "con"), None, None), check_vma=False
    )
```

profile of v0, /device:TPU:1, one launch (start us, length us, event | category | flops | bytes accessed | tf_op | source)
XLA Modules:
  0.0 249.5 jit_solution(3944979912727412526)
XLA Ops:
  6.5 0.7 convert_reduce_fusion
  7.3 0.8 dynamic_slice.7
  8.1 1.0 fusion.14
  9.0 1.6 compare_select_fusion
  10.7 0.0 all-gather.2.cloned.1.call-update
  10.7 0.0 reduce-scatter.2.cloned.1.call-start
  10.8 86.7 %all-gather.2.cloned.1.call-done = bf16[512,8,800]{2,0,1:T(8,128)(2,1)} async-done(((bf16[8,8,800]{2,0,1:T(8,128)(2,1)}), bf16[512,8,800]{2,0,1:T(8,128)(2,1)}) %all-gather.2.cloned.1.call-update) | async-done | bytes 6553616 | tf_op jit(solution)/shard_map/all_gather | solution.py:48
  97.5 15.9 %fusion.7 = f32[512,64,16]{0,1,2:T(8,128)S(1)} fusion(bf16[256,16,800]{0,2,1:T(8,128)(2,1)} %param.13, bf16[512,8,800]{2,0,1:T(8,128)(2,1)} %all-gather.2.cloned.1.call-done, bf16[256,64,8]{0,2,1:T(8,128)(2,1)} %param.12), kind=kOutput, calls=%fused_computation.5 | convolution fusion | flops 10072883200 | bytes 15466496 | tf_op jit(solution)/shard_map/pcd,acbd->pab/dot_general | solution.py:46
  113.4 3.8 %copy.29 = f32[512,64,16]{1,2,0:T(8,128)} copy(f32[512,64,16]{0,1,2:T(8,128)S(1)} %fusion.7) | data formatting | bytes 4194304 | tf_op jit(solution)/shard_map/pcd,acbd->pab/dot_general | solution.py:46
  117.2 4.6 %reshape.33 = f32[64,1,8192]{2,1,0:T(1,128)S(1)} reshape(f32[512,16,64]{2,1,0:T(8,128)} %bitcast.28) | data formatting | bytes 4194304
  121.7 55.4 %all_to_all.18 = f32[64,1,8192]{2,1,0:T(1,128)} all-to-all(f32[64,1,8192]{2,1,0:T(1,128)S(1)} %reshape.33), channel_id=1, replica_groups=mesh['idx'=64,'con'=4] {'idx'}, dimensions={0} | all-to-all | bytes 4194304 | tf_op jit(solution)/shard_map/all_to_all | solution.py:52
  177.2 0.5 broadcast.37
  177.7 7.6 %reduce = f32[64,8192]{1,0:T(8,128)S(1)} reduce(f32[64,1,8192]{2,1,0:T(1,128)} %all_to_all.18, f32[]{:T(128)} %broadcast.37), dimensions={1}, to_apply=%all_to_all.13.reduce_sub_computation | reduce | bytes 4194308 | tf_op jit(solution)/shard_map/all_to_all | solution.py:52
  185.3 3.0 %reshape.34 = f32[512,16,64]{2,1,0:T(8,128)} reshape(f32[64,8192]{1,0:T(8,128)S(1)} %reduce) | data formatting | bytes 4194304
  188.3 4.6 %copy.30 = f32[8,64,64,16]{1,3,2,0:T(8,128)} copy(f32[8,64,64,16]{1,3,0,2:T(8,128)} %bitcast.30) | data formatting | bytes 4194304 | tf_op jit(solution)/shard_map/all_to_all | solution.py:52
  192.9 0.8 dynamic_slice.6
  193.7 0.1 broadcast_in_dim.8
  193.8 0.1 eq.43
  193.9 0.1 broadcast_in_dim.9
  193.9 0.1 reshape.28
  194.0 0.7 fusion.17
  194.7 45.4 %reduce-scatter.2.cloned.1.call-done = f32[2,64,1024]{1,2,0:T(8,128)} async-done(((f32[8,64,1024]{1,2,0:T(8,128)}), f32[2,64,1024]{1,2,0:T(8,128)}) %reduce-scatter.2.cloned.1.call-update) | async-done | bytes 524304 | tf_op jit(solution)/shard_map/reduce_scatter | solution.py:53
  240.1 1.5 and_select_fusion
  241.6 1.1 copy.31
  (12 shorter events, 0.0 us)
Async XLA Ops:
  6.5 1.5 copy-start
  6.5 91.0 %all-gather.2.cloned.1.call-start = ((), (), s32[]{:S(2)}) async-start(), calls=%async_computation.2 | async-start | bytes 7454720 | tf_op jit(solution)/shard_map/all_gather | solution.py:48
  10.7 229.4 %reduce-scatter.2.cloned.1.call-start = ((), (), s32[]{:S(2)}) async-start(), calls=%async_computation.3 | async-start | bytes 5242880 | tf_op jit(solution)/shard_map/reduce_scatter | solution.py:53
  188.3 5.4 %copy-start.1 = (s32[64]{0:T(128)S(1)}, s32[64]{0:T(128)}, u32[]{:S(2)}) copy-start(s32[64]{0:T(128)} %param.19) | copy-start | bytes 772
  188.3 5.5 %copy-start.2 = (s32[64]{0:T(128)S(1)}, s32[64]{0:T(128)}, u32[]{:S(2)}) copy-start(s32[64]{0:T(128)} %param.18) | copy-start | bytes 772
  188.3 5.7 %copy-start.3 = (s32[64]{0:T(128)S(1)}, s32[64]{0:T(128)}, u32[]{:S(2)}) copy-start(s32[64]{0:T(128)} %param.14) | copy-start | bytes 772
Sparse Core Ops, SparseCore 0:
  10.8 86.6 all-gather.1
  193.1 46.9 reduce-scatter.1
where the time goes:
time: 250 us
  waiting for transfers between devices  132 us (53%)
  blocking collectives  55.4 us (22%)
  local copies, waits for them, and re-layouts  19.4 us (8%)
  matrix products  17.5 us (7%)
  between operations  13.5 us (5%)
  other arithmetic  11.5 us (5%)
    all_gather x1, waiting for transfers between devices, body(): lax.all_gather(masked, 'idx', axis=0, tiled=True)  86.7 us
    all_to_all x1, blocking collectives, body(): lax.all_to_all(partial_value, 'idx', split_axis=0, concat_axis=2, tiled=T...  55.4 us
    reduce_scatter x1, waiting for transfers between devices, body(): summed = lax.psum_scatter(moved, 'con', scatter_dimension=0, tiled=True)  45.4 us
    dot_general x1, matrix products, body(): jnp.einsum('pcd,acbd->pab', lax.all_gather(masked, 'idx', axis=0, tiled=T...  15.9 us
    all_to_all x1, other arithmetic, body(): lax.all_to_all(partial_value, 'idx', split_axis=0, concat_axis=2, tiled=T...  7.63 us
    unnamed x10, local copies, waits for them, and re-layouts  7.61 us
    all_to_all x2, local copies, waits for them, and re-layouts, body(): lax.all_to_all(partial_value, 'idx', split_axis=0, concat_axis=2, tiled=T...  5.07 us
  transfers between devices with their start and end apart: 2, of which 2 were waited for; matrix products, arithmetic and copies ran while one was open for 1% of the time, Pallas kernels for 0%

commit v1 on v0

v1 whole, which is shorter than its diff:
```python
import functools

import jax
import jax.numpy as jnp
from jax import lax
from jax.experimental import pallas as pl
from jax.experimental.pallas import tpu as pltpu
from jax.sharding import PartitionSpec as P

MESH = pl.DeviceIdType.MESH
BW = 16
NIRR = 8
WIN = 192
SLOTS = 16
NV = 800
KDIM = 8 * WIN
F32 = jnp.float32
BF16 = jnp.bfloat16


def nt_dot(left, right):
    return lax.dot_general(left, right, (((1,), (1,)), ((), ())), preferred_element_type=F32)


def lookup(index, entries):
    out = jnp.zeros_like(index)
    for spot, entry in enumerate(entries):
        out = jnp.where(index == spot, entry, out)
    return out


def ladder_kernel(
    pair_s, airr_s, cirr_s, start_s, prod_s, tirr_s, round_s,
    amp_ref, a_ref, pairs_ref, f_hbm,
    out_ref,
    fv, x32, tc, tsend, trecv, g_ref, asel, d_ref, rhs, rneed, acc, xf, xb, xr, m_ref, v0, v1,
    fsem, tsib_s, tsib_r, y_s, y_r, rr_s, rr_r, rl_s, rl_r, sib_s, sib_r, x_s, x_r, a_s, a_r, v_s, v_r,
):
    idx = lax.axis_index("idx")
    con = lax.axis_index("con")
    core = lax.rem(idx, 2)
    chip = idx // 2
    y = lax.rem(chip, 4)
    z = chip // 4
    sibling = (chip * 2 + 1 - core, con)

    def chip_at(zz, yy):
        return ((zz * 4 + yy) * 2 + core, con)

    for b in range(16):
        pltpu.make_async_copy(f_hbm.at[b], fv.at[b], fsem.at[b]).start()

    barrier = pltpu.get_barrier_semaphore()
    pl.semaphore_signal(barrier, inc=1, device_id=sibling, device_id_type=MESH)

    def greet(j, carry):
        other = lax.rem(chip + j, 32)
        pl.semaphore_signal(barrier, inc=1, device_id=(other * 2 + core, con), device_id_type=MESH)
        return carry

    lax.fori_loop(1, 32, greet, 0)
    for s in range(1, 4):
        pl.semaphore_signal(barrier, inc=1, device_id=(idx, lax.rem(con + s, 4)), device_id_type=MESH)

    first = [jnp.minimum(start_s[g] // 32, (NV - WIN) // 32) for g in range(NIRR)]
    base = [first[g] * 32 for g in range(NIRR)]
    low = [start_s[g] - base[g] for g in range(NIRR)]
    high = [(start_s[g + 1] if g < 7 else NV) - base[g] for g in range(NIRR)]
    x32[:, 768:896] = jnp.zeros((64, 128), F32)
    x32[:, 0:NV] = amp_ref[...].astype(F32).reshape(64, NV)
    rows8 = lax.broadcasted_iota(jnp.int32, (8, 128), 0)
    target = []
    for p in range(8):
        irr = pair_s[idx * 8 + p]
        part = jnp.zeros((8, 128), jnp.int32)
        for c in range(8):
            part = jnp.where(rows8 == c, prod_s[irr, cirr_s[c]], part)
        target.append(part)
    target = jnp.concatenate(target, axis=0)
    target = jnp.concatenate([target, target], axis=1)
    lanes = lax.broadcasted_iota(jnp.int32, (64, 256), 1)
    window = jnp.zeros((64, 256), F32)
    whole = x32[...]
    for g in range(NIRR):
        moved = pltpu.roll(whole, 896 - base[g], 1)[:, 0:256]
        window = jnp.where((target == g) & (lanes >= low[g]) & (lanes < high[g]), moved, window)
    tc[0, :, :] = window[:, 0:128]
    tc[1, :, :] = window[:, 128:256]
    lane8 = lax.broadcasted_iota(jnp.int32, (8, 128), 1)
    for c in range(8):
        tsend[:, c * 128:(c + 1) * 128] = tc[0, pl.ds(c, 8, stride=8), :]
    for m in range(4):
        even = tc[1, pl.ds(2 * m, 8, stride=8), :]
        odd = pltpu.roll(tc[1, pl.ds(2 * m + 1, 8, stride=8), :], 64, 1)
        tsend[:, 1024 + m * 128:1024 + (m + 1) * 128] = jnp.where(lane8 < 64, even, odd)

    pl.semaphore_wait(barrier, 35)
    tcopy = pltpu.make_async_remote_copy(
        src_ref=tsend, dst_ref=trecv, send_sem=tsib_s, recv_sem=tsib_r, device_id=sibling, device_id_type=MESH)
    tcopy.start()

    tile = tirr_s[idx]
    prow = [[prod_s[i, j] for j in range(8)] for i in range(8)]
    ptile = [prod_s[i, tile] for i in range(8)]
    n = lax.broadcasted_iota(jnp.int32, (8, 512), 1)
    a_of, c_of = n // 8, lax.rem(n, 8)
    a_lane = lookup(a_of, [airr_s[a] for a in range(64)])
    c_lane = lookup(c_of, [cirr_s[c] for c in range(8)])
    a_rows = []
    for k in range(8):
        part = jnp.zeros((8, 128), jnp.int32)
        for i in range(8):
            part = jnp.where(rows8 == i, airr_s[k * 8 + i], part)
        a_rows.append(part)
    rank = jnp.zeros((8, 512), jnp.int32)
    for k in range(8):
        other = jnp.concatenate([a_rows[k]] * 4, axis=1)
        rank = rank + jnp.where((other == a_lane) & (lax.broadcasted_iota(jnp.int32, (8, 512), 0) + k * 8 < a_of), 1, 0)
    rank = jnp.sum(rank, axis=0, keepdims=True) - round_s[0] * SLOTS
    block = lookup(lookup(a_lane, ptile) * 8 + c_lane, [e for row in prow for e in row])[0:1]
    code = jnp.where((rank >= 0) & (rank < SLOTS), block * 128 + c_of[0:1] * SLOTS + rank, -1)
    spot = lax.broadcasted_iota(jnp.int32, (128, 512), 0)
    for g in range(NIRR):
        pick = jnp.where(spot + g * 128 == code, 1.0, 0.0).astype(BF16)
        asel[g, :, :] = jnp.dot(pick, a_ref[...], preferred_element_type=F32).astype(BF16)

    need = lookup(lookup(pairs_ref[...], ptile), list(range(8))).astype(F32)
    eye = lax.broadcasted_iota(jnp.int32, (128, 128), 0) == lax.broadcasted_iota(jnp.int32, (128, 128), 1)
    for k in range(4):
        column = jnp.sum(jnp.where(eye, need[k:k + 1, :], 0.0), axis=1, keepdims=True)
        rneed[pl.ds(k * 128, 128), :] = jnp.broadcast_to(column, (128, 128))

    def integrals(begin, end):
        def one(b, carry):
            for g in range(NIRR):
                main = fv[b, pl.ds(first[g], 6), :, :].reshape(WIN, 256)
                tail = fv[b, pl.ds(first[g] + 4, 2), :, :].reshape(64, 256)
                got = nt_dot(asel[g], jnp.concatenate([main, tail], axis=0))
                d_ref[g, :, pl.ds(pl.multiple_of(b * 16, 16), 16), :] = got.astype(BF16).reshape(8, 16, 256)
            return carry

        lax.fori_loop(begin, end, one, 0)

    half = pl.ds(pl.multiple_of(core * 768, 128), 768)

    def group(zz):
        return g_ref.at[pl.ds(pl.multiple_of(lax.rem(zz + 8, 8) * 64, 64), 64), half]

    def to_sibling(slot, zz):
        part = group(zz)
        return pltpu.make_async_remote_copy(
            src_ref=part, dst_ref=part, send_sem=sib_s.at[slot], recv_sem=sib_r.at[slot], device_id=sibling, device_id_type=MESH)

    def ring(zz, to, send, recv):
        part = group(zz)
        return pltpu.make_async_remote_copy(
            src_ref=part, dst_ref=part, send_sem=send, recv_sem=recv, device_id=chip_at(lax.rem(to + 8, 8), y), device_id_type=MESH)

    def right(s):
        return ring(z - s, z + 1, rr_s.at[s], rr_r.at[s])

    def right_in(s):
        return ring(z - 1 - s, z + 1, rr_s.at[s], rr_r.at[s])

    def left(s):
        return ring(z + s, z - 1, rl_s.at[s], rl_r.at[s])

    def left_in(s):
        return ring(z + 1 + s, z - 1, rl_s.at[s], rl_r.at[s])

    for b in range(16):
        pltpu.make_async_copy(f_hbm.at[b], fv.at[b], fsem.at[b]).wait()
    integrals(0, 1)
    tcopy.wait()
    own, other = tsend[...], trecv[...]
    top = jnp.where(core == 0, own[:, 0:768], other[:, 768:KDIM])
    bottom = jnp.where(core == 0, other[:, 0:768], own[:, 768:KDIM])
    mine = pl.ds(pl.multiple_of(chip * 16, 16), 16)
    g_ref[mine, half] = jnp.concatenate([top, bottom], axis=0).astype(BF16)

    def along_y(s):
        part = g_ref.at[mine, half]
        return pltpu.make_async_remote_copy(
            src_ref=part, dst_ref=part, send_sem=y_s.at[s - 1], recv_sem=y_r.at[s - 1],
            device_id=chip_at(z, lax.rem(y + s, 4)), device_id_type=MESH)

    def along_y_in(s):
        part = g_ref.at[pl.ds(pl.multiple_of((z * 4 + lax.rem(y + 4 - s, 4)) * 16, 16), 16), half]
        return pltpu.make_async_remote_copy(
            src_ref=part, dst_ref=part, send_sem=y_s.at[s - 1], recv_sem=y_r.at[s - 1],
            device_id=chip_at(z, lax.rem(y + s, 4)), device_id_type=MESH)

    for s in range(1, 4):
        along_y(s).start()
    integrals(1, 3)
    for s in range(1, 4):
        along_y_in(s).wait_recv()
    right(0).start()
    left(0).start()
    to_sibling(0, z).start()
    integrals(3, 6)
    right_in(0).wait_recv()
    right(1).start()
    left_in(0).wait_recv()
    left(1).start()
    to_sibling(1, z - 1).start()
    to_sibling(2, z + 1).start()
    integrals(6, 10)
    right_in(1).wait_recv()
    right(2).start()
    left_in(1).wait_recv()
    left(2).start()
    to_sibling(3, z - 2).start()
    to_sibling(4, z + 2).start()
    integrals(10, 14)
    right_in(2).wait_recv()
    right(3).start()
    left_in(2).wait_recv()
    to_sibling(5, z - 3).start()
    to_sibling(6, z + 3).start()
    integrals(14, 16)
    right_in(3).wait_recv()
    to_sibling(7, z - 4).start()

    other_half = pl.ds(pl.multiple_of((1 - core) * 768, 128), 768)
    for slot, away in enumerate((0, -1, 1, -2, 2, -3, 3, -4)):
        part = g_ref.at[pl.ds(pl.multiple_of(lax.rem(z + away + 8, 8) * 64, 64), 64), other_half]
        pltpu.make_async_remote_copy(
            src_ref=part, dst_ref=part, send_sem=sib_s.at[slot], recv_sem=sib_r.at[slot], device_id=sibling,
            device_id_type=MESH).wait_recv()

    acc[...] = jnp.zeros_like(acc)
    lane256 = lax.broadcasted_iota(jnp.int32, (256, 128), 1)

    def one_irrep(r, carry):
        pair_irr = prod_s[r, tile]
        blocks = [prod_s[pair_irr, cirr_s[c]] for c in range(8)]
        for c in range(8):
            rhs[:, c * 128:(c + 1) * 128] = d_ref[blocks[c], c, :, 0:128]
        for m in range(4):
            even = d_ref[blocks[2 * m], 2 * m, :, 128:256]
            odd = d_ref[blocks[2 * m + 1], 2 * m + 1, :, 128:256]
            rhs[:, 1024 + m * 128:1024 + (m + 1) * 128] = jnp.where(lane256 < 64, even, odd)
        for k in range(2):
            rows = pl.ds(k * 256, 256)
            got = nt_dot(g_ref[rows, :], rhs[...])
            hit = rneed[rows, :] == r.astype(F32)
            for h in range(2):
                acc[h, rows, :] = jnp.where(hit, got[:, h * 128:(h + 1) * 128], acc[h, rows, :])
        return carry

    lax.fori_loop(0, NIRR, one_irrep, 0)

    for r in range(4):
        for q in range(4):
            for h in range(2):
                for cg in range(4):
                    xf[r, pl.ds(cg * 64 + q * 2 + h, 8, stride=8), :] = acc[
                        h, pl.ds(cg * 128 + (q // 2) * 8 + r * 2 + q % 2, 8, stride=16), :]
        xb[r, :, :] = xf[r, :, :].astype(BF16)

    def along_x(s):
        to = lax.rem(con + s, 4)
        return pltpu.make_async_remote_copy(
            src_ref=xb.at[to], dst_ref=xr.at[s - 1], send_sem=x_s.at[s - 1], recv_sem=x_r.at[s - 1],
            device_id=(idx, to), device_id_type=MESH)

    for s in range(1, 4):
        along_x(s).start()
    for s in range(1, 4):
        along_x(s).wait_recv()
    m_ref[...] = xf[con, :, :] + (xr[0].astype(F32) + xr[1].astype(F32) + xr[2].astype(F32))

    here = pl.ds(pl.multiple_of(chip * 8, 8), 8)

    def give(j, carry):
        other_chip = lax.rem(chip + j, 32)
        pltpu.make_async_remote_copy(
            src_ref=m_ref.at[pl.ds(pl.multiple_of(other_chip * 8, 8), 8), :], dst_ref=v0.at[here, :], send_sem=a_s, recv_sem=a_r,
            device_id=(other_chip * 2 + core, con), device_id_type=MESH).start()
        return carry

    lax.fori_loop(1, 32, give, 0)
    v0[here, :] = m_ref[here, :]
    many = v0.at[0:248, :]
    pltpu.make_async_copy(many, many, a_r).wait()
    vcopy = pltpu.make_async_remote_copy(
        src_ref=v0, dst_ref=v1, send_sem=v_s, recv_sem=v_r, device_id=sibling, device_id_type=MESH)
    vcopy.start()
    out_ref[core, :, :] = v0[...]
    pltpu.make_async_copy(many, many, a_s).wait()
    for s in range(1, 4):
        along_y(s).wait_send()
        along_x(s).wait_send()
    for s in range(4):
        right(s).wait_send()
    for s in range(3):
        left(s).wait_send()
    for slot in range(8):
        to_sibling(slot, z).wait_send()
    vcopy.wait()
    out_ref[1 - core, :, :] = v1[...]


def place_kernel(
    pair_s, prod_s, round_s, airr_ref, tlen_ref, tirr_ref, v_ref, prev_ref, out_ref, left, expand, *, first_round
):
    idx = lax.axis_index("idx")
    con = lax.axis_index("con")
    core = lax.rem(idx, 2)
    lane16 = lax.broadcasted_iota(jnp.int32, (16, 128), 1)
    for h in range(2):
        parts = []
        for pp in range(2):
            for kappa in range(2):
                parts.append(v_ref[kappa, pl.ds(core * 4 + pp * 2 + h, 32, stride=8), :])
        turned = jnp.concatenate(parts, axis=0).T
        for bl in range(8):
            piece = turned[bl * 16:(bl + 1) * 16, :]
            for pp in range(2):
                kept = jnp.where((lane16 // 64) == pp, piece, 0.0)
                left[pl.ds(pp * 16, 16), (h * 8 + bl) * 128:(h * 8 + bl + 1) * 128] = kept
    source = lax.broadcasted_iota(jnp.int32, (128, 1024), 0)
    lane = lax.broadcasted_iota(jnp.int32, (128, 1024), 1)
    local = lax.rem(source, 64)
    tile_first = (lax.rem(local, 32) * 2 + local // 32) * 16
    for b in range(16):
        expand[b * 128:(b + 1) * 128, :] = jnp.where(tile_first + b == lane, 1.0, 0.0).astype(BF16)
    a_row = airr_ref[...]
    row = lax.broadcasted_iota(jnp.int32, (64, 64), 0)
    col = lax.broadcasted_iota(jnp.int32, (64, 64), 1)
    a_col = jnp.sum(jnp.where(row == col, a_row, 0), axis=1, keepdims=True)
    rank = jnp.sum(jnp.where((a_col == a_row) & (col < row), 1, 0), axis=1, keepdims=True) - round_s[0] * SLOTS
    slot = lax.broadcasted_iota(jnp.int32, (64, 32), 1)
    full = left[...]
    big = full.astype(BF16)
    small = (full - big.astype(F32)).astype(BF16)
    held = (rank >= 0) & (rank < SLOTS)
    pick = [jnp.where(held & (slot == rank + pp * 16), 1.0, 0.0) for pp in range(2)]
    pick = jnp.concatenate(pick, axis=0).astype(BF16)
    table = expand[...]

    def placed(part):
        chosen = jnp.dot(pick, part, preferred_element_type=F32).astype(BF16)
        return jnp.dot(chosen, table, preferred_element_type=F32)

    values = placed(big) + placed(small)
    spread = jnp.where(
        lax.broadcasted_iota(jnp.int32, (64, 1024), 0) == lax.broadcasted_iota(jnp.int32, (64, 1024), 1) // 16, 1.0, 0.0
    ).astype(BF16)

    def lanes_of(ref):
        wide = jnp.broadcast_to(ref[...], (8, 64)).astype(F32).astype(BF16)
        return jnp.dot(wide, spread, preferred_element_type=F32)[0:1]

    length, irrep = lanes_of(tlen_ref), lanes_of(tirr_ref).astype(jnp.int32)
    live = lax.rem(lax.broadcasted_iota(jnp.int32, (1, 1024), 1), 16).astype(F32) < length
    for pp in range(2):
        pair_irr = pair_s[idx * 8 + con * 2 + pp]
        need = lookup(irrep, [prod_s[pair_irr, i] for i in range(8)])
        need = jnp.where(live, need, -1)
        keep = a_col == need
        got = jnp.where(keep, values[pp * 64:(pp + 1) * 64, :], 0.0)
        if not first_round:
            got = got + prev_ref[pp, :, :]
        out_ref[pp, :, :] = got


def smem():
    return pl.BlockSpec(memory_space=pltpu.SMEM)


def vmem():
    return pl.BlockSpec(memory_space=pltpu.VMEM)


def ladder(pair_irrep, a_irrep, c_irrep, irrep_start, product, tile_irrep, number, amplitude, fit, pairs, fitting):
    dma = pltpu.SemaphoreType.DMA
    return pl.pallas_call(
        ladder_kernel,
        out_shape=jax.ShapeDtypeStruct((2, 256, 128), F32),
        in_specs=[smem()] * 7 + [vmem()] * 3 + [pl.BlockSpec(memory_space=pltpu.HBM)],
        out_specs=vmem(),
        scratch_shapes=[
            pltpu.VMEM((16, 25, 32, 256), BF16),
            pltpu.VMEM((64, 896), F32),
            pltpu.VMEM((2, 64, 128), F32),
            pltpu.VMEM((8, KDIM), F32),
            pltpu.VMEM((8, KDIM), F32),
            pltpu.VMEM((512, KDIM), BF16),
            pltpu.VMEM((NIRR, 128, 256), BF16),
            pltpu.VMEM((NIRR, 8, 256, 256), BF16),
            pltpu.VMEM((256, KDIM), BF16),
            pltpu.VMEM((512, 128), F32),
            pltpu.VMEM((2, 512, 128), F32),
            pltpu.VMEM((4, 256, 128), F32),
            pltpu.VMEM((4, 256, 128), BF16),
            pltpu.VMEM((3, 256, 128), BF16),
            pltpu.VMEM((256, 128), F32),
            pltpu.VMEM((256, 128), F32),
            pltpu.VMEM((256, 128), F32),
            dma((16,)), dma, dma, dma((3,)), dma((3,)), dma((4,)), dma((4,)), dma((3,)), dma((3,)),
            dma((8,)), dma((8,)), dma((3,)), dma((3,)), dma, dma, dma, dma,
        ],
        compiler_params=pltpu.CompilerParams(
            collective_id=0, has_side_effects=True, vmem_limit_bytes=48 * 1024 * 1024),
        name="ladder",
    )(pair_irrep, a_irrep, c_irrep, irrep_start, product, tile_irrep, number, amplitude, fit, pairs, fitting)


def place(pair_irrep, product, number, a_irrep, tile_len, tile_irrep, gathered, previous, first_round):
    return pl.pallas_call(
        functools.partial(place_kernel, first_round=first_round),
        out_shape=jax.ShapeDtypeStruct((2, 64, 1024), F32),
        in_specs=[smem()] * 3 + [vmem()] * 5,
        out_specs=vmem(),
        scratch_shapes=[pltpu.VMEM((32, 2048), F32), pltpu.VMEM((2048, 1024), BF16)],
        compiler_params=pltpu.CompilerParams(vmem_limit_bytes=48 * 1024 * 1024),
        name="place" if first_round else "place_more",
    )(pair_irrep, product, number, a_irrep, tile_len, tile_irrep, gathered, previous)


def body(
    amplitude, pair_irrep, fit_ac, fitting_tensor_bd, a_irrep, c_irrep, irrep_start, product, tile_len, tile_irrep
):
    fitting = jnp.transpose(fitting_tensor_bd, (1, 2, 0)).reshape(16, 25, 32, 256)
    fit = jnp.transpose(fit_ac, (1, 2, 0)).reshape(512, 256)
    pairs = pair_irrep.reshape(4, 128)
    a_row, len_row, irr_row = a_irrep.reshape(1, 64), tile_len.reshape(1, 64), tile_irrep.reshape(1, 64)
    counts = jnp.sum((a_irrep[:, None] == jnp.arange(NIRR, dtype=jnp.int32)[None, :]).astype(jnp.int32), axis=0)
    rounds = (jnp.max(counts) + SLOTS - 1) // SLOTS

    def one_round(number, previous, first_round):
        number = jnp.asarray(number, jnp.int32).reshape(1)
        gathered = ladder(
            pair_irrep, a_irrep, c_irrep, irrep_start, product, tile_irrep, number, amplitude, fit, pairs, fitting)
        return place(pair_irrep, product, number, a_row, len_row, irr_row, gathered, previous, first_round)

    out = one_round(0, jnp.zeros((2, 64, 1024), F32), False)

    def more(carry):
        return carry[0] < rounds

    def step(carry):
        number, out = carry
        return number + 1, one_round(number, out, False)

    return lax.while_loop(more, step, (jnp.int32(1), out))[1]


def solution(mesh):
    placed = (
        P("idx", None, None),
        P(),
        P("con", None, None),
        P("con", "idx", None),
        P(),
        P(),
        P(),
        P(),
        P(),
        P(),
    )
    return jax.shard_map(
        body, mesh=mesh, in_specs=placed, out_specs=P(("idx", "con"), None, None), check_vma=False
    )
```

time: 250 us -> 62.2 us (0.25)
  waiting for transfers between devices: 132 us -> 0 us
  Pallas kernels: 0 us -> 58.6 us
  blocking collectives: 55.4 us -> 0 us
  local copies, waits for them, and re-layouts: 19.4 us -> 0.88 us
  matrix products: 17.5 us -> 0 us
  between operations: 13.5 us -> 0.84 us
  other arithmetic: 11.5 us -> 1.57 us
    all_gather x1 -> x0, waiting for transfers between devices: 86.7 us -> none  [body(): lax.all_gather(masked, 'idx', axis=0, tiled=True)]
    pallas_call x0 -> x2, Pallas kernels: none -> 58.6 us  [the longest x1 55.5 us: ladder(): pl.pallas_call(ladder_kernel, out_shape=jax.ShapeDtypeStruct((2, 256, 128...]
    all_to_all x1 -> x0, blocking collectives: 55.4 us -> none  [body(): lax.all_to_all(partial_value, 'idx', split_axis=0, concat_axis=2, tiled=T...]
    reduce_scatter x1 -> x0, waiting for transfers between devices: 45.4 us -> none  [body(): summed = lax.psum_scatter(moved, 'con', scatter_dimension=0, tiled=True)]
    dot_general x3 -> x0, matrix products: 17.5 us -> none  [the longest x1 15.9 us: body(): jnp.einsum('pcd,acbd->pab', lax.all_gather(masked, 'idx', axis=0, tiled=T...]
    all_to_all x1 -> x0, other arithmetic: 7.63 us -> none  [body(): lax.all_to_all(partial_value, 'idx', split_axis=0, concat_axis=2, tiled=T...]
    unnamed x10 -> x20, local copies, waits for them, and re-layouts: 7.61 us -> 0.83 us
    all_to_all x2 -> x0, local copies, waits for them, and re-layouts: 5.07 us -> none  [body(): lax.all_to_all(partial_value, 'idx', split_axis=0, concat_axis=2, tiled=T...]
  transfers between devices with their start and end apart: 2 -> 0, of which waited for: 2 -> 0; matrix products, arithmetic and copies ran while one was open for 1% -> 0% of each run, Pallas kernels for 0% -> 0%
where the time goes in v1:
time: 62.2 us; the launch traced here: 62.1 us
  Pallas kernels  58.6 us (94%)
  other arithmetic  1.57 us (3%)
  local copies, waits for them, and re-layouts  0.88 us (1%)
  between operations  0.84 us (1%)
    pallas_call x1, Pallas kernels, ladder(): pl.pallas_call(ladder_kernel, out_shape=jax.ShapeDtypeStruct((2, 256, 128...  55.5 us
    pallas_call x1, Pallas kernels, place(): pl.pallas_call(functools.partial(place_kernel, first_round=first_round),...  3.14 us

profile of v1, /device:TPU:1, one launch (start us, length us, event | category | flops | bytes accessed | tf_op | source)
XLA Modules:
  0.0 62.1 jit_solution(8450871313006349600)
XLA Ops:
  0.0 0.0 copy-start.5
  0.0 0.0 copy-start.1
  0.0 0.0 copy-start.2
  0.0 0.0 copy-start.8
  0.0 0.0 copy-start.9
  0.0 0.0 copy-start.4
  0.1 0.0 copy-start.6
  0.1 0.0 copy-start.7
  0.1 0.9 %convert_reduce_fusion = s32[8]{0:T(128)S(1)} fusion(s32[64]{0:T(128)} %airr_s.1), kind=kLoop, calls=%fused_computation | loop fusion | flops 1528 | bytes 288 | tf_op jit(solution)/shard_map/reduce_sum | solution.py:430
  1.0 0.6 %reduce_max.9 = s32[]{:T(128)} reduce(s32[8]{0:T(128)S(1)} %convert_reduce_fusion, s32[]{:T(128)} %constant.24.clone.1), dimensions={0}, to_apply=%region_1.0 | reduce | flops 7 | bytes 40 | tf_op jit(solution)/shard_map/reduce_max | solution.py:431
  2.3 55.5 %ladder.2.v_ref = f32[2,256,128]{2,1,0:T(8,128)S(1)} custom-call(s32[512]{0:T(512)} %pair_s.3, s32[64]{0:T(128)} %airr_s.1, s32[8]{0:T(128)} %cirr_s.1, s32[8]{0:T(128)} %start_s.1, s32[8,8]{1,0:T(8,128)} %prod_s.3, s32[64]{0:T(128)} %tirr_s.1, s32[1]{0:T(128)} %constant.21.clone.1.round_s, bf16[8,8,800]{2,1,0:T(8,128)(2,1)} %amp_ref.1, ...), custom_call_target="tpu_custom_call" | custom-call | tf_op jit(solution)/shard_map/ladder/pallas_call | solution.py:379
  57.9 0.0 copy-done.5
  57.9 0.0 copy-done.3
  57.9 0.0 copy-done.4
  57.9 0.0 copy-done.6
  57.9 0.0 copy-done.7
  57.9 3.1 %place_more.2 = f32[2,64,1024]{2,1,0:T(8,128)S(1)} custom-call(s32[512]{0:T(512)S(1)} %copy-done.3, s32[8,8]{1,0:T(8,128)S(1)} %copy-done.4, s32[1]{0:T(128)} %constant.21.clone.1.round_s, s32[1,64]{1,0:T(1,128)S(1)} %bitcast.22, s32[1,64]{1,0:T(1,128)S(1)} %bitcast.30, s32[1,64]{1,0:T(1,128)S(1)} %bitcast.26, f32[2,256,128]{2,1,0:T(8,128)S(1)} %ladder.2.v_ref, ...), custom_call_target="tpu_custom_call" | custom-call | tf_op jit(solution)/shard_map/place_more/pallas_call | solution.py:412
  61.1 0.0 copy-done.1
  61.1 0.0 copy-done.2
  61.1 0.0 copy-done.8
  61.1 0.0 copy-done.9
  61.1 0.2 while.10
  61.3 0.0 copy-start
  61.3 0.8 %copy-done = f32[2,64,1024]{2,1,0:T(8,128)} copy-done((f32[2,64,1024]{2,1,0:T(8,128)}, f32[2,64,1024]{2,1,0:T(8,128)S(1)}, u32[]{:S(2)}) %copy-start) | copy-done | bytes 524312
  (2 shorter events, 0.0 us)
Async XLA Ops:
  0.0 57.9 %copy-start.5 = (s32[64]{0:T(128)S(1)}, s32[64]{0:T(128)}, u32[]{:S(2)}) copy-start(s32[64]{0:T(128)} %airr_s.1) | copy-start | bytes 772
  0.0 61.1 %copy-start.1 = (bf16[256,64,8]{0,2,1:T(8,128)(2,1)S(1)}, bf16[256,64,8]{0,2,1:T(8,128)(2,1)}, u32[]{:S(2)}) copy-start(bf16[256,64,8]{0,2,1:T(8,128)(2,1)} %param.14) | copy-start | bytes 786436
  0.0 57.9 %copy-start.3 = (s32[512]{0:T(512)S(1)}, s32[512]{0:T(512)}, u32[]{:S(2)}) copy-start(s32[512]{0:T(512)} %pair_s.3) | copy-start | bytes 6148
  0.0 61.1 %copy-start.2 = (bf16[8,8,800]{2,1,0:T(8,128)(2,1)S(1)}, bf16[8,8,800]{2,1,0:T(8,128)(2,1)}, u32[]{:S(2)}) copy-start(bf16[8,8,800]{2,1,0:T(8,128)(2,1)} %amp_ref.1) | copy-start | bytes 307204
  0.0 61.1 %copy-start.8 = (s32[8]{0:T(128)S(1)}, s32[8]{0:T(128)}, u32[]{:S(2)}) copy-start(s32[8]{0:T(128)} %cirr_s.1) | copy-start | bytes 100
  0.0 61.1 %copy-start.9 = (s32[8]{0:T(128)S(1)}, s32[8]{0:T(128)}, u32[]{:S(2)}) copy-start(s32[8]{0:T(128)} %start_s.1) | copy-start | bytes 100
  0.0 57.9 %copy-start.4 = (s32[8,8]{1,0:T(8,128)S(1)}, s32[8,8]{1,0:T(8,128)}, u32[]{:S(2)}) copy-start(s32[8,8]{1,0:T(8,128)} %prod_s.3) | copy-start | bytes 772
  0.1 57.8 %copy-start.6 = (s32[64]{0:T(128)S(1)}, s32[64]{0:T(128)}, u32[]{:S(2)}) copy-start(s32[64]{0:T(128)} %tirr_s.1) | copy-start | bytes 772
  0.1 57.8 %copy-start.7 = (s32[64]{0:T(128)S(1)}, s32[64]{0:T(128)}, u32[]{:S(2)}) copy-start(s32[64]{0:T(128)} %param.20) | copy-start | bytes 772
  61.3 0.8 %copy-start = (f32[2,64,1024]{2,1,0:T(8,128)}, f32[2,64,1024]{2,1,0:T(8,128)S(1)}, u32[]{:S(2)}) copy-start(f32[2,64,1024]{2,1,0:T(8,128)S(1)} %get-tuple-element.270) | copy-start | bytes 1572868

commit v2 on v1

v2 whole, which is shorter than its diff:
```python
import functools

import jax
import jax.numpy as jnp
from jax import lax
from jax.experimental import pallas as pl
from jax.experimental.pallas import tpu as pltpu
from jax.sharding import PartitionSpec as P

MESH = pl.DeviceIdType.MESH
BW = 16
NIRR = 8
WIN = 192
SLOTS = 16
NV = 800
KDIM = 8 * WIN
CUT = 384
F32 = jnp.float32
BF16 = jnp.bfloat16


def nt_dot(left, right):
    return lax.dot_general(left, right, (((1,), (1,)), ((), ())), preferred_element_type=F32)


def lookup(index, entries):
    out = jnp.zeros_like(index)
    for spot, entry in enumerate(entries):
        out = jnp.where(index == spot, entry, out)
    return out


def ladder_kernel(
    pair_s, airr_s, cirr_s, start_s, prod_s, tirr_s, round_s,
    amp_ref, a_ref, pairs_ref, f_hbm,
    out_ref,
    fv, x32, tc, tsend, trecv, g_ref, asel, d_ref, rhs, rneed, acc, xf, xb, xr, zf, zb, vb,
    fsem, tsib_s, tsib_r, y_s, y_r, rr_s, rr_r, rl_s, rl_r, sib_s, sib_r, zg_s, zg_r, side_s, side_r, on_s, on_r,
    x_s, x_r, ze_s, ze_r,
):
    idx = lax.axis_index("idx")
    con = lax.axis_index("con")
    core = lax.rem(idx, 2)
    chip = idx // 2
    y = lax.rem(chip, 4)
    z = chip // 4
    sibling = (chip * 2 + 1 - core, con)

    def at_y(dy):
        return ((z * 4 + lax.rem(y + dy + 4, 4)) * 2 + core, con)

    def at_z(dz):
        return ((lax.rem(z + dz + 8, 8) * 4 + y) * 2 + core, con)

    def at_x(dx):
        return (idx, lax.rem(con + dx, 4))

    def remote(src, dst, send, recv, to):
        return pltpu.make_async_remote_copy(
            src_ref=src, dst_ref=dst, send_sem=send, recv_sem=recv, device_id=to, device_id_type=MESH)

    for b in range(16):
        pltpu.make_async_copy(f_hbm.at[b], fv.at[b], fsem.at[b]).start()

    barrier = pltpu.get_barrier_semaphore()
    peers = [sibling]
    for s in range(1, 8):
        there = lax.rem(z + s, 8) * 4 + y
        peers += [(there * 2 + core, con), (there * 2 + 1 - core, con)]
    for s in range(4):
        for dx in range(4):
            if s or dx:
                peers.append(((z * 4 + lax.rem(y + s, 4)) * 2 + core, lax.rem(con + dx, 4)))
    for peer in peers:
        pl.semaphore_signal(barrier, inc=1, device_id=peer, device_id_type=MESH)

    first = [jnp.minimum(start_s[g] // 32, (NV - WIN) // 32) for g in range(NIRR)]
    base = [first[g] * 32 for g in range(NIRR)]
    low = [start_s[g] - base[g] for g in range(NIRR)]
    high = [(start_s[g + 1] if g < 7 else NV) - base[g] for g in range(NIRR)]
    x32[:, 768:896] = jnp.zeros((64, 128), F32)
    x32[:, 0:NV] = amp_ref[...].astype(F32).reshape(64, NV)
    rows8 = lax.broadcasted_iota(jnp.int32, (8, 128), 0)
    target = []
    for p in range(8):
        irr = pair_s[idx * 8 + p]
        part = jnp.zeros((8, 128), jnp.int32)
        for c in range(8):
            part = jnp.where(rows8 == c, prod_s[irr, cirr_s[c]], part)
        target.append(part)
    target = jnp.concatenate(target, axis=0)
    target = jnp.concatenate([target, target], axis=1)
    lanes = lax.broadcasted_iota(jnp.int32, (64, 256), 1)
    window = jnp.zeros((64, 256), F32)
    whole = x32[...]
    for g in range(NIRR):
        moved = pltpu.roll(whole, 896 - base[g], 1)[:, 0:256]
        window = jnp.where((target == g) & (lanes >= low[g]) & (lanes < high[g]), moved, window)
    tc[0, :, :] = window[:, 0:128]
    tc[1, :, :] = window[:, 128:256]
    lane8 = lax.broadcasted_iota(jnp.int32, (8, 128), 1)
    for c in range(8):
        tsend[:, c * 128:(c + 1) * 128] = tc[0, pl.ds(c, 8, stride=8), :]
    for m in range(4):
        even = tc[1, pl.ds(2 * m, 8, stride=8), :]
        odd = pltpu.roll(tc[1, pl.ds(2 * m + 1, 8, stride=8), :], 64, 1)
        tsend[:, 1024 + m * 128:1024 + (m + 1) * 128] = jnp.where(lane8 < 64, even, odd)

    pl.semaphore_wait(barrier, len(peers))
    tcopy = remote(tsend, trecv, tsib_s, tsib_r, sibling)
    tcopy.start()

    tile = tirr_s[idx]
    prow = [[prod_s[i, j] for j in range(8)] for i in range(8)]
    ptile = [prod_s[i, tile] for i in range(8)]

    def factors():
        n = lax.broadcasted_iota(jnp.int32, (8, 512), 1)
        a_of, c_of = n // 8, lax.rem(n, 8)
        a_lane = lookup(a_of, [airr_s[a] for a in range(64)])
        c_lane = lookup(c_of, [cirr_s[c] for c in range(8)])
        a_rows = []
        for k in range(8):
            part = jnp.zeros((8, 128), jnp.int32)
            for i in range(8):
                part = jnp.where(rows8 == i, airr_s[k * 8 + i], part)
            a_rows.append(part)
        rank = jnp.zeros((8, 512), jnp.int32)
        for k in range(8):
            other = jnp.concatenate([a_rows[k]] * 4, axis=1)
            rank = rank + jnp.where(
                (other == a_lane) & (lax.broadcasted_iota(jnp.int32, (8, 512), 0) + k * 8 < a_of), 1, 0)
        rank = jnp.sum(rank, axis=0, keepdims=True) - round_s[0] * SLOTS
        block = lookup(lookup(a_lane, ptile) * 8 + c_lane, [e for row in prow for e in row])[0:1]
        code = jnp.where((rank >= 0) & (rank < SLOTS), block * 128 + c_of[0:1] * SLOTS + rank, -1)
        spot = lax.broadcasted_iota(jnp.int32, (128, 512), 0)
        for g in range(NIRR):
            pick = jnp.where(spot + g * 128 == code, 1.0, 0.0).astype(BF16)
            asel[g, :, :] = jnp.dot(pick, a_ref[...], preferred_element_type=F32).astype(BF16)

    def needs():
        need = lookup(lookup(pairs_ref[...], ptile), list(range(8))).astype(F32)
        eye = lax.broadcasted_iota(jnp.int32, (128, 128), 0) == lax.broadcasted_iota(jnp.int32, (128, 128), 1)
        for k in range(4):
            column = jnp.sum(jnp.where(eye, need[k:k + 1, :], 0.0), axis=1, keepdims=True)
            column = jnp.broadcast_to(column, (128, 128))
            for j in range(8):
                zz, yy = 2 * k + j // 4, j % 4
                rneed[pl.ds(yy * 128 + zz * 16, 16), :] = column[j * 16:(j + 1) * 16, :]

    def integrals(begin, end):
        def one(b, carry):
            for g in range(NIRR):
                main = fv[b, pl.ds(first[g], 6), :, :].reshape(WIN, 256)
                tail = fv[b, pl.ds(first[g] + 4, 2), :, :].reshape(64, 256)
                got = nt_dot(asel[g], jnp.concatenate([main, tail], axis=0))
                d_ref[g, :, pl.ds(pl.multiple_of(b * 16, 16), 16), :] = got.astype(BF16).reshape(8, 16, 256)
            return carry

        lax.fori_loop(begin, end, one, 0)

    lanes_a, lanes_b = pl.ds(0, CUT), pl.ds(CUT, KDIM - CUT)

    def unit(dz, dy, lanes):
        return g_ref.at[lax.rem(y + dy + 4, 4), lax.rem(z + dz + 8, 8), :, lanes]

    def group(dz, lanes):
        return g_ref.at[:, lax.rem(z + dz + 8, 8), :, lanes]

    away = (0, -1, 1, -2, 2, -3, 3, -4)

    def to_sibling(dz, lanes):
        slot = away.index(dz)
        return remote(group(dz, lanes), group(dz, lanes), sib_s.at[slot], sib_r.at[slot], sibling)

    def along_y(s):
        return remote(unit(0, 0, lanes_a), unit(0, 0, lanes_a), y_s.at[s - 1], y_r.at[s - 1], at_y(s))

    def along_y_in(s):
        return remote(unit(0, -s, lanes_a), unit(0, -s, lanes_a), y_s.at[s - 1], y_r.at[s - 1], at_y(s))

    def right(dz, s):
        return remote(group(dz, lanes_a), group(dz, lanes_a), rr_s.at[s], rr_r.at[s], at_z(1))

    def left(dz, s):
        return remote(group(dz, lanes_a), group(dz, lanes_a), rl_s.at[s], rl_r.at[s], at_z(-1))

    def along_z(s):
        return remote(unit(0, 0, lanes_b), unit(0, 0, lanes_b), zg_s.at[s - 1], zg_r.at[s - 1], at_z(s))

    def along_z_in(dz):
        s = (-dz) % 8
        return remote(unit(dz, 0, lanes_b), unit(dz, 0, lanes_b), zg_s.at[s - 1], zg_r.at[s - 1], at_z(s))

    def side(dz, dy):
        slot, way = away.index(dz), (dy + 1) // 2
        part = unit(dz, 0, lanes_b)
        return remote(part, part, side_s.at[slot, way], side_r.at[slot, way], at_y(dy))

    def side_in(dz, dy):
        slot, way = away.index(dz), (dy + 1) // 2
        part = unit(dz, -dy, lanes_b)
        return remote(part, part, side_s.at[slot, way], side_r.at[slot, way], at_y(dy))

    def onward(dz):
        slot, dy = away.index(dz), (1 if dz % 2 == 0 else -1)
        part = unit(dz, -dy, lanes_b)
        return remote(part, part, on_s.at[slot], on_r.at[slot], at_y(dy))

    def onward_in(dz):
        slot, dy = away.index(dz), (1 if dz % 2 == 0 else -1)
        part = unit(dz, 2, lanes_b)
        return remote(part, part, on_s.at[slot], on_r.at[slot], at_y(dy))

    def route_a(stage):
        if stage == 0:
            for s in range(1, 4):
                along_y(s).start()
            return
        if stage == 1:
            for s in range(1, 4):
                along_y_in(s).wait_recv()
            right(0, 0).start()
            left(0, 0).start()
            to_sibling(0, lanes_a).start()
            return
        if stage > 5:
            return
        right(1 - stage, stage - 2).wait_recv()
        if stage < 5:
            right(1 - stage, stage - 1).start()
            left(stage - 1, stage - 2).wait_recv()
            if stage < 4:
                left(stage - 1, stage - 1).start()
            to_sibling(1 - stage, lanes_a).start()
            to_sibling(stage - 1, lanes_a).start()
        else:
            to_sibling(-4, lanes_a).start()

    def both(far):
        return (-4,) if far == 4 else (0,) if far == 0 else (-far, far)

    def route_b(stage):
        if stage == 0:
            for s in (1, 7, 2, 6, 3, 5, 4):
                along_z(s).start()
        if stage <= 4:
            for dz in both(stage):
                if dz != 0:
                    along_z_in(dz).wait_recv()
                side(dz, 1).start()
                side(dz, -1).start()
        if 0 <= stage - 1 <= 4:
            for dz in both(stage - 1):
                side_in(dz, 1).wait_recv()
                side_in(dz, -1).wait_recv()
                onward(dz).start()
        if 0 <= stage - 2 <= 4:
            for dz in both(stage - 2):
                onward_in(dz).wait_recv()
                to_sibling(dz, lanes_b).start()

    def gather(stage):
        @pl.when(core == 0)
        def _():
            route_a(stage)

        @pl.when(core == 1)
        def _():
            route_b(stage)

    factors()
    tcopy.wait()
    own, other = tsend[...], trecv[...]
    @pl.when(core == 0)
    def _():
        g_ref[y, z, :, lanes_a] = jnp.concatenate([own[:, 0:CUT], other[:, 0:CUT]], axis=0).astype(BF16)

    @pl.when(core == 1)
    def _():
        g_ref[y, z, :, lanes_b] = jnp.concatenate([other[:, CUT:KDIM], own[:, CUT:KDIM]], axis=0).astype(BF16)

    gather(0)
    needs()
    for b in range(16):
        pltpu.make_async_copy(f_hbm.at[b], fv.at[b], fsem.at[b]).wait()
    done = 0
    for stage, until in ((1, 2), (2, 5), (3, 8), (4, 11), (5, 14), (6, 16)):
        integrals(done, until)
        done = until
        gather(stage)

    lane256 = lax.broadcasted_iota(jnp.int32, (256, 128), 1)
    for r in range(NIRR):
        blocks = [prod_s[prod_s[r, tile], cirr_s[c]] for c in range(8)]
        for c in range(8):
            rhs[r, :, c * 128:(c + 1) * 128] = d_ref[blocks[c], c, :, 0:128]
        for m in range(4):
            even = d_ref[blocks[2 * m], 2 * m, :, 128:256]
            odd = d_ref[blocks[2 * m + 1], 2 * m + 1, :, 128:256]
            rhs[r, :, 1024 + m * 128:1024 + (m + 1) * 128] = jnp.where(lane256 < 64, even, odd)

    @pl.when(core == 0)
    def _():
        for dz in away:
            to_sibling(dz, lanes_b).wait_recv()

    @pl.when(core == 1)
    def _():
        for dz in away:
            to_sibling(dz, lanes_a).wait_recv()

    def give(to, dx):
        other = lax.rem(con + dx, 4)
        return remote(
            xb.at[to, other], xr.at[y, dx], x_s.at[to, dx], x_r.at[y, dx], ((z * 4 + to) * 2 + core, other))

    def given(src, dx):
        return remote(xb.at[src, con], xr.at[src, dx], x_s.at[src, dx], x_r.at[src, dx], at_x(dx))

    for h in range(2):
        rows = pl.ds(h * 256, 256)
        left_side = g_ref[2 * h:2 * h + 2].reshape(256, KDIM)
        for r in range(NIRR):
            got = nt_dot(left_side, rhs[r])
            for k in range(2):
                part = got[:, k * 128:(k + 1) * 128]
                acc[k, rows, :] = part if r == 0 else jnp.where(rneed[rows, :] == float(r), part, acc[k, rows, :])
        for j in range(2):
            to = 2 * h + j
            for r in range(4):
                for q in range(4):
                    for k in range(2):
                        xf[pl.ds(r * 64 + q * 2 + k, 8, stride=8), :] = acc[
                            k, pl.ds(to * 128 + (q // 2) * 8 + r * 2 + q % 2, 8, stride=16), :]
            xb[to, :, :, :] = xf[...].astype(BF16).reshape(4, 64, 128)
            for dx in range(1, 4):
                give(to, dx).start()

            @pl.when(y != to)
            def _():
                give(to, 0).start()

    xr[y, 0, :, :] = xb[y, con, :, :]
    for src in range(4):
        @pl.when(y != src)
        def _():
            given(src, 0).wait_recv()

        for dx in range(1, 4):
            given(src, dx).wait_recv()
        total = (xr[src, 0].astype(F32) + xr[src, 1].astype(F32)) + (xr[src, 2].astype(F32) + xr[src, 3].astype(F32))
        for zz in range(8):
            for k in range(2):
                zf[zz, k, src * 4:(src + 1) * 4, :] = total[zz * 8 + k * 4:zz * 8 + k * 4 + 4, :]
    zb[...] = zf[...].astype(BF16)

    def own_z(s, flip):
        to = lax.rem(z + s, 8)
        kk = 1 - core if flip else core
        return remote(
            zb.at[to, kk], vb.at[core, z], ze_s.at[s, flip], ze_r.at[s, flip], ((to * 4 + y) * 2 + kk, con))

    def own_z_in(s, flip):
        src = lax.rem(z + 8 - s, 8)
        kk = 1 - core if flip else core
        return remote(
            zb.at[src, kk], vb.at[kk, src], ze_s.at[s, flip], ze_r.at[s, flip], ((src * 4 + y) * 2 + kk, con))

    routes = [(s, flip) for s in (4, 3, 5, 2, 6, 1, 7, 0) for flip in (0, 1) if (s, flip) != (0, 0)]
    for s, flip in routes:
        own_z(s, flip).start()
    vb[core, z, :, :] = zb[z, core, :, :]
    for s, flip in routes:
        own_z_in(s, flip).wait_recv()
    out_ref[...] = vb[...]

    @pl.when(core == 0)
    def _():
        for s in range(1, 4):
            along_y(s).wait_send()
        for s in range(4):
            right(-s, s).wait_send()
        for s in range(3):
            left(s, s).wait_send()
        for dz in away:
            to_sibling(dz, lanes_a).wait_send()

    @pl.when(core == 1)
    def _():
        for s in range(1, 8):
            along_z(s).wait_send()
        for dz in away:
            side(dz, 1).wait_send()
            side(dz, -1).wait_send()
            onward(dz).wait_send()
            to_sibling(dz, lanes_b).wait_send()

    for to in range(4):
        for dx in range(1, 4):
            give(to, dx).wait_send()

        @pl.when(y != to)
        def _():
            give(to, 0).wait_send()

    for s, flip in routes:
        own_z(s, flip).wait_send()


def place_kernel(
    pair_s, prod_s, round_s, airr_ref, tlen_ref, tirr_ref, v_ref, prev_ref, out_ref, rounds_s, v32, left, expand, *, first_round
):
    idx = lax.axis_index("idx")
    con = lax.axis_index("con")
    lane16 = lax.broadcasted_iota(jnp.int32, (16, 128), 1)
    v32[...] = v_ref[...].reshape(2, 128, 128).astype(F32)
    for h in range(2):
        parts = []
        for pp in range(2):
            for kappa in range(2):
                parts.append(v32[kappa, pl.ds(pp * 2 + h, 32, stride=4), :])
        turned = jnp.concatenate(parts, axis=0).T
        for bl in range(8):
            piece = turned[bl * 16:(bl + 1) * 16, :]
            for pp in range(2):
                kept = jnp.where((lane16 // 64) == pp, piece, 0.0)
                left[pl.ds(pp * 16, 16), (h * 8 + bl) * 128:(h * 8 + bl + 1) * 128] = kept
    source = lax.broadcasted_iota(jnp.int32, (128, 1024), 0)
    lane = lax.broadcasted_iota(jnp.int32, (128, 1024), 1)
    local = lax.rem(source, 64)
    tile_first = (lax.rem(local, 32) * 2 + local // 32) * 16
    for b in range(16):
        expand[b * 128:(b + 1) * 128, :] = jnp.where(tile_first + b == lane, 1.0, 0.0).astype(BF16)
    a_row = airr_ref[...]
    row = lax.broadcasted_iota(jnp.int32, (64, 64), 0)
    col = lax.broadcasted_iota(jnp.int32, (64, 64), 1)
    a_col = jnp.sum(jnp.where(row == col, a_row, 0), axis=1, keepdims=True)
    rank = jnp.sum(jnp.where((a_col == a_row) & (col < row), 1, 0), axis=1, keepdims=True)
    rounds_s[0] = jnp.max(rank) // SLOTS + 1
    rank = rank - round_s[0] * SLOTS
    slot = lax.broadcasted_iota(jnp.int32, (64, 32), 1)
    full = left[...].astype(BF16)
    held = (rank >= 0) & (rank < SLOTS)
    pick = [jnp.where(held & (slot == rank + pp * 16), 1.0, 0.0) for pp in range(2)]
    pick = jnp.concatenate(pick, axis=0).astype(BF16)
    chosen = jnp.dot(pick, full, preferred_element_type=F32).astype(BF16)
    values = jnp.dot(chosen, expand[...], preferred_element_type=F32)
    spread = jnp.where(
        lax.broadcasted_iota(jnp.int32, (64, 1024), 0) == lax.broadcasted_iota(jnp.int32, (64, 1024), 1) // 16, 1.0, 0.0
    ).astype(BF16)

    def lanes_of(ref):
        wide = jnp.broadcast_to(ref[...], (8, 64)).astype(F32).astype(BF16)
        return jnp.dot(wide, spread, preferred_element_type=F32)[0:1]

    length, irrep = lanes_of(tlen_ref), lanes_of(tirr_ref).astype(jnp.int32)
    live = lax.rem(lax.broadcasted_iota(jnp.int32, (1, 1024), 1), 16).astype(F32) < length
    for pp in range(2):
        pair_irr = pair_s[idx * 8 + con * 2 + pp]
        need = lookup(irrep, [prod_s[pair_irr, i] for i in range(8)])
        need = jnp.where(live, need, -1)
        keep = a_col == need
        got = jnp.where(keep, values[pp * 64:(pp + 1) * 64, :], 0.0)
        if not first_round:
            got = got + prev_ref[pp, :, :]
        out_ref[pp, :, :] = got


def smem():
    return pl.BlockSpec(memory_space=pltpu.SMEM)


def vmem():
    return pl.BlockSpec(memory_space=pltpu.VMEM)


def ladder(pair_irrep, a_irrep, c_irrep, irrep_start, product, tile_irrep, number, amplitude, fit, pairs, fitting):
    dma = pltpu.SemaphoreType.DMA
    return pl.pallas_call(
        ladder_kernel,
        out_shape=jax.ShapeDtypeStruct((2, 8, 16, 128), BF16),
        in_specs=[smem()] * 7 + [vmem()] * 3 + [pl.BlockSpec(memory_space=pltpu.HBM)],
        out_specs=vmem(),
        scratch_shapes=[
            pltpu.VMEM((16, 25, 32, 256), BF16),
            pltpu.VMEM((64, 896), F32),
            pltpu.VMEM((2, 64, 128), F32),
            pltpu.VMEM((8, KDIM), F32),
            pltpu.VMEM((8, KDIM), F32),
            pltpu.VMEM((4, 8, 16, KDIM), BF16),
            pltpu.VMEM((NIRR, 128, 256), BF16),
            pltpu.VMEM((NIRR, 8, 256, 256), BF16),
            pltpu.VMEM((NIRR, 256, KDIM), BF16),
            pltpu.VMEM((512, 128), F32),
            pltpu.VMEM((2, 512, 128), F32),
            pltpu.VMEM((256, 128), F32),
            pltpu.VMEM((4, 4, 64, 128), BF16),
            pltpu.VMEM((4, 4, 64, 128), BF16),
            pltpu.VMEM((8, 2, 16, 128), F32),
            pltpu.VMEM((8, 2, 16, 128), BF16),
            pltpu.VMEM((2, 8, 16, 128), BF16),
            dma((16,)), dma, dma, dma((3,)), dma((3,)), dma((4,)), dma((4,)), dma((3,)), dma((3,)),
            dma((8,)), dma((8,)), dma((7,)), dma((7,)), dma((8, 2)), dma((8, 2)), dma((8,)), dma((8,)),
            dma((4, 4)), dma((4, 4)), dma((8, 2)), dma((8, 2)),
        ],
        compiler_params=pltpu.CompilerParams(
            collective_id=0, has_side_effects=True, vmem_limit_bytes=48 * 1024 * 1024),
        name="ladder",
    )(pair_irrep, a_irrep, c_irrep, irrep_start, product, tile_irrep, number, amplitude, fit, pairs, fitting)


def place(pair_irrep, product, number, a_irrep, tile_len, tile_irrep, gathered, previous, first_round):
    return pl.pallas_call(
        functools.partial(place_kernel, first_round=first_round),
        out_shape=(jax.ShapeDtypeStruct((2, 64, 1024), F32), jax.ShapeDtypeStruct((1,), jnp.int32)),
        in_specs=[smem()] * 3 + [vmem()] * 5,
        out_specs=(vmem(), smem()),
        scratch_shapes=[pltpu.VMEM((2, 128, 128), F32), pltpu.VMEM((32, 2048), F32), pltpu.VMEM((2048, 1024), BF16)],
        compiler_params=pltpu.CompilerParams(vmem_limit_bytes=48 * 1024 * 1024),
        name="place" if first_round else "place_more",
    )(pair_irrep, product, number, a_irrep, tile_len, tile_irrep, gathered, previous)


def body(
    amplitude, pair_irrep, fit_ac, fitting_tensor_bd, a_irrep, c_irrep, irrep_start, product, tile_len, tile_irrep
):
    fitting = jnp.transpose(fitting_tensor_bd, (1, 2, 0)).reshape(16, 25, 32, 256)
    fit = jnp.transpose(fit_ac, (1, 2, 0)).reshape(512, 256)
    pairs = pair_irrep.reshape(4, 128)
    a_row, len_row, irr_row = a_irrep.reshape(1, 64), tile_len.reshape(1, 64), tile_irrep.reshape(1, 64)
    def one_round(number, previous, first_round):
        number = jnp.asarray(number, jnp.int32).reshape(1)
        gathered = ladder(
            pair_irrep, a_irrep, c_irrep, irrep_start, product, tile_irrep, number, amplitude, fit, pairs, fitting)
        return place(pair_irrep, product, number, a_row, len_row, irr_row, gathered, previous, first_round)

    out, rounds = one_round(0, jnp.zeros((2, 64, 1024), F32), False)

    def more(carry):
        return carry[0] < rounds[0]

    def step(carry):
        number, out = carry
        return number + 1, one_round(number, out, False)[0]

    return lax.while_loop(more, step, (jnp.int32(1), out))[1]


def solution(mesh):
    placed = (
        P("idx", None, None),
        P(),
        P("con", None, None),
        P("con", "idx", None),
        P(),
        P(),
        P(),
        P(),
        P(),
        P(),
    )
    return jax.shard_map(
        body, mesh=mesh, in_specs=placed, out_specs=P(("idx", "con"), None, None), check_vma=False
    )
```

time: 62.2 us -> 49.5 us (0.80)
  Pallas kernels: 58.6 us -> 47.5 us
  other arithmetic: 1.57 us -> 0 us
  between operations: 0.84 us -> 0.16 us
  loops' own time: 0.19 us -> 0.82 us
    pallas_call x1, Pallas kernels: 55.5 us -> 45.3 us  [ladder(): pl.pallas_call(ladder_kernel, out_shape=jax.ShapeDtypeStruct((2, 8, 16, 1...]
    reduce_sum x1 -> x0, other arithmetic: 0.93 us -> none  [body(): jnp.sum((a_irrep[:, None] == jnp.arange(NIRR, dtype=jnp.int32)[None, :])....]
    pallas_call x1, Pallas kernels: 3.14 us -> 2.25 us  [place(): pl.pallas_call(functools.partial(place_kernel, first_round=first_round),...]
    reduce_max x1 -> x0, other arithmetic: 0.64 us -> none  [body(): rounds = (jnp.max(counts) + SLOTS - 1) // SLOTS]
    another operation x1, loops' own time: 0.19 us -> 0.82 us  [body(): return lax.while_loop(more, step, (jnp.int32(1), out))[1]]
where the time goes in v2:
time: 49.5 us; the launch traced here: 49.4 us
  Pallas kernels  47.5 us (96%)
  local copies, waits for them, and re-layouts  0.87 us (2%)
  loops' own time  0.82 us (2%)
    pallas_call x1, Pallas kernels, ladder(): pl.pallas_call(ladder_kernel, out_shape=jax.ShapeDtypeStruct((2, 8, 16, 1...  45.3 us
    pallas_call x1, Pallas kernels, place(): pl.pallas_call(functools.partial(place_kernel, first_round=first_round),...  2.25 us

profile of v2, /device:TPU:1, one launch (start us, length us, event | category | flops | bytes accessed | tf_op | source)
XLA Modules:
  0.0 49.4 jit_solution(1231058212909863300)
XLA Ops:
  0.0 0.0 copy-start.1
  0.0 0.0 copy-start.3
  0.0 0.0 copy-start.2
  0.0 0.0 copy-start.5
  0.0 0.0 copy-start.8
  0.0 0.0 copy-start.9
  0.0 0.0 copy-start.4
  0.0 0.0 copy-start.6
  0.1 0.0 copy-start.7
  0.1 45.3 %ladder.2.v_ref = bf16[2,8,16,128]{3,2,1,0:T(8,128)(2,1)S(1)} custom-call(s32[512]{0:T(512)} %pair_s.3, s32[64]{0:T(128)} %airr_s.1, s32[8]{0:T(128)} %cirr_s.1, s32[8]{0:T(128)} %start_s.1, s32[8,8]{1,0:T(8,128)} %prod_s.3, s32[64]{0:T(128)} %tirr_s.1, s32[1]{0:T(128)} %constant.2.clone.1.round_s, bf16[8,8,800]{2,1,0:T(8,128)(2,1)} %amp_ref.1, ...), custom_call_target="tpu_custom_call" | custom-call | tf_op jit(solution)/shard_map/ladder/pallas_call | solution.py:480
  45.4 0.0 copy-done.3
  45.4 0.0 copy-done.5
  45.4 0.0 copy-done.4
  45.4 0.0 copy-done.6
  45.4 0.0 copy-done.7
  45.4 2.3 %place_more.2 = (f32[2,64,1024]{2,1,0:T(8,128)S(1)}, s32[1]{0:T(128)}) custom-call(s32[512]{0:T(512)S(1)} %copy-done.3, s32[8,8]{1,0:T(8,128)S(1)} %copy-done.4, s32[1]{0:T(128)} %constant.2.clone.1.round_s, s32[1,64]{1,0:T(1,128)S(1)} %bitcast.24, s32[1,64]{1,0:T(1,128)S(1)} %bitcast.32, s32[1,64]{1,0:T(1,128)S(1)} %bitcast.28, ...), custom_call_target="tpu_custom_call" | custom-call | tf_op jit(solution)/shard_map/place_more/pallas_call | solution.py:514
  47.7 0.0 copy-done.1
  47.7 0.0 copy-done.2
  47.7 0.0 copy-done.8
  47.7 0.0 copy-done.9
  47.7 0.8 %while.10 = (s32[]{:T(128)}, f32[2,64,1024]{2,1,0:T(8,128)S(1)}, s32[1]{0:T(128)}, s32[512]{0:T(512)S(1)}, s32[64]{0:T(128)S(1)}, /*index=5*/s32[8]{0:T(128)S(1)...) while((s32[]{:T(128)}, f32[2,64,1024]{2,1,0:T(8,128)S(1)}, ...), condition=%wide.region_1.0_spmd, body=%wide.region_0.0_spmd.sunk | while | flops 2 | bytes 1048733 | solution.py:547
  48.6 0.0 copy-start
  48.6 0.8 %copy-done = f32[2,64,1024]{2,1,0:T(8,128)} copy-done((f32[2,64,1024]{2,1,0:T(8,128)}, f32[2,64,1024]{2,1,0:T(8,128)S(1)}, u32[]{:S(2)}) %copy-start) | copy-done | bytes 524312
  (1 shorter events, 0.0 us)
Async XLA Ops:
  0.0 47.7 %copy-start.1 = (bf16[256,64,8]{0,2,1:T(8,128)(2,1)S(1)}, bf16[256,64,8]{0,2,1:T(8,128)(2,1)}, u32[]{:S(2)}) copy-start(bf16[256,64,8]{0,2,1:T(8,128)(2,1)} %param.14) | copy-start | bytes 786436
  0.0 45.4 %copy-start.3 = (s32[512]{0:T(512)S(1)}, s32[512]{0:T(512)}, u32[]{:S(2)}) copy-start(s32[512]{0:T(512)} %pair_s.3) | copy-start | bytes 6148
  0.0 47.7 %copy-start.2 = (bf16[8,8,800]{2,1,0:T(8,128)(2,1)S(1)}, bf16[8,8,800]{2,1,0:T(8,128)(2,1)}, u32[]{:S(2)}) copy-start(bf16[8,8,800]{2,1,0:T(8,128)(2,1)} %amp_ref.1) | copy-start | bytes 307204
  0.0 45.4 %copy-start.5 = (s32[64]{0:T(128)S(1)}, s32[64]{0:T(128)}, u32[]{:S(2)}) copy-start(s32[64]{0:T(128)} %airr_s.1) | copy-start | bytes 772
  0.0 47.7 %copy-start.8 = (s32[8]{0:T(128)S(1)}, s32[8]{0:T(128)}, u32[]{:S(2)}) copy-start(s32[8]{0:T(128)} %cirr_s.1) | copy-start | bytes 100
  0.0 47.7 %copy-start.9 = (s32[8]{0:T(128)S(1)}, s32[8]{0:T(128)}, u32[]{:S(2)}) copy-start(s32[8]{0:T(128)} %start_s.1) | copy-start | bytes 100
  0.0 45.4 %copy-start.4 = (s32[8,8]{1,0:T(8,128)S(1)}, s32[8,8]{1,0:T(8,128)}, u32[]{:S(2)}) copy-start(s32[8,8]{1,0:T(8,128)} %prod_s.3) | copy-start | bytes 772
  0.0 45.4 %copy-start.6 = (s32[64]{0:T(128)S(1)}, s32[64]{0:T(128)}, u32[]{:S(2)}) copy-start(s32[64]{0:T(128)} %tirr_s.1) | copy-start | bytes 772
  0.1 45.4 %copy-start.7 = (s32[64]{0:T(128)S(1)}, s32[64]{0:T(128)}, u32[]{:S(2)}) copy-start(s32[64]{0:T(128)} %param.20) | copy-start | bytes 772
  48.6 0.8 %copy-start = (f32[2,64,1024]{2,1,0:T(8,128)}, f32[2,64,1024]{2,1,0:T(8,128)S(1)}, u32[]{:S(2)}) copy-start(f32[2,64,1024]{2,1,0:T(8,128)S(1)} %get-tuple-element.277) | copy-start | bytes 1572868

commit v3 on v2

--- a/solution.py
+++ b/solution.py
@@ -14,7 +14,7 @@
 SLOTS = 16
 NV = 800
 KDIM = 8 * WIN
-CUT = 384
+CUT = 256
 F32 = jnp.float32
 BF16 = jnp.bfloat16
 
@@ -34,8 +34,8 @@
     pair_s, airr_s, cirr_s, start_s, prod_s, tirr_s, round_s,
     amp_ref, a_ref, pairs_ref, f_hbm,
     out_ref,
-    fv, x32, tc, tsend, trecv, g_ref, asel, d_ref, rhs, rneed, acc, xf, xb, xr, zf, zb, vb,
-    fsem, tsib_s, tsib_r, y_s, y_r, rr_s, rr_r, rl_s, rl_r, sib_s, sib_r, zg_s, zg_r, side_s, side_r, on_s, on_r,
+    fv, x32, tc, tsend, trecv, ga, gb, asel, d_ref, rhs, rneed, acc, xf, xb, xr, zf, zb, vb,
+    fsem, tsib_s, tsib_r, y_s, y_r, gz_s, gz_r, sib_s, sib_r, one_s, one_r, zg_s, zg_r, side_s, side_r, on_s, on_r,
     x_s, x_r, ze_s, ze_r,
 ):
     idx = lax.axis_index("idx")
@@ -144,9 +144,8 @@
         for k in range(4):
             column = jnp.sum(jnp.where(eye, need[k:k + 1, :], 0.0), axis=1, keepdims=True)
             column = jnp.broadcast_to(column, (128, 128))
-            for j in range(8):
-                zz, yy = 2 * k + j // 4, j % 4
-                rneed[pl.ds(yy * 128 + zz * 16, 16), :] = column[j * 16:(j + 1) * 16, :]
+            rneed[2 * k, :, :] = column[0:64, :]
+            rneed[2 * k + 1, :, :] = column[64:128, :]
 
     def integrals(begin, end):
         def one(b, carry):
@@ -159,57 +158,63 @@
 
         lax.fori_loop(begin, end, one, 0)
 
-    lanes_a, lanes_b = pl.ds(0, CUT), pl.ds(CUT, KDIM - CUT)
-
-    def unit(dz, dy, lanes):
-        return g_ref.at[lax.rem(y + dy + 4, 4), lax.rem(z + dz + 8, 8), :, lanes]
-
-    def group(dz, lanes):
-        return g_ref.at[:, lax.rem(z + dz + 8, 8), :, lanes]
+    def unit_a(dy):
+        return ga.at[z, lax.rem(y + dy + 4, 4)]
+
+    def group_a(dz):
+        return ga.at[lax.rem(z + dz + 8, 8)]
+
+    def unit(dz, dy):
+        return gb.at[lax.rem(y + dy + 4, 4), lax.rem(z + dz + 8, 8)]
 
     away = (0, -1, 1, -2, 2, -3, 3, -4)
 
-    def to_sibling(dz, lanes):
+    def to_sibling(dz):
         slot = away.index(dz)
-        return remote(group(dz, lanes), group(dz, lanes), sib_s.at[slot], sib_r.at[slot], sibling)
+        return remote(group_a(dz), group_a(dz), sib_s.at[slot], sib_r.at[slot], sibling)
+
+    def unit_to_sibling(dz, dy):
+        slot, part = away.index(dz), unit(dz, dy)
+        return remote(part, part, one_s.at[slot, dy % 4], one_r.at[slot, dy % 4], sibling)
 
     def along_y(s):
-        return remote(unit(0, 0, lanes_a), unit(0, 0, lanes_a), y_s.at[s - 1], y_r.at[s - 1], at_y(s))
+        return remote(unit_a(0), unit_a(0), y_s.at[s - 1], y_r.at[s - 1], at_y(s))
 
     def along_y_in(s):
-        return remote(unit(0, -s, lanes_a), unit(0, -s, lanes_a), y_s.at[s - 1], y_r.at[s - 1], at_y(s))
-
-    def right(dz, s):
-        return remote(group(dz, lanes_a), group(dz, lanes_a), rr_s.at[s], rr_r.at[s], at_z(1))
-
-    def left(dz, s):
-        return remote(group(dz, lanes_a), group(dz, lanes_a), rl_s.at[s], rl_r.at[s], at_z(-1))
+        return remote(unit_a(-s), unit_a(-s), y_s.at[s - 1], y_r.at[s - 1], at_y(s))
+
+    def groups_z(s):
+        return remote(group_a(0), group_a(0), gz_s.at[s - 1], gz_r.at[s - 1], at_z(s))
+
+    def groups_z_in(dz):
+        s = (-dz) % 8
+        return remote(group_a(dz), group_a(dz), gz_s.at[s - 1], gz_r.at[s - 1], at_z(s))
 
     def along_z(s):
-        return remote(unit(0, 0, lanes_b), unit(0, 0, lanes_b), zg_s.at[s - 1], zg_r.at[s - 1], at_z(s))
+        return remote(unit(0, 0), unit(0, 0), zg_s.at[s - 1], zg_r.at[s - 1], at_z(s))
 
     def along_z_in(dz):
         s = (-dz) % 8
-        return remote(unit(dz, 0, lanes_b), unit(dz, 0, lanes_b), zg_s.at[s - 1], zg_r.at[s - 1], at_z(s))
+        return remote(unit(dz, 0), unit(dz, 0), zg_s.at[s - 1], zg_r.at[s - 1], at_z(s))
 
     def side(dz, dy):
         slot, way = away.index(dz), (dy + 1) // 2
-        part = unit(dz, 0, lanes_b)
+        part = unit(dz, 0)
         return remote(part, part, side_s.at[slot, way], side_r.at[slot, way], at_y(dy))
 
     def side_in(dz, dy):
         slot, way = away.index(dz), (dy + 1) // 2
-        part = unit(dz, -dy, lanes_b)
+        part = unit(dz, -dy)
         return remote(part, part, side_s.at[slot, way], side_r.at[slot, way], at_y(dy))
 
     def onward(dz):
         slot, dy = away.index(dz), (1 if dz % 2 == 0 else -1)
-        part = unit(dz, -dy, lanes_b)
+        part = unit(dz, -dy)
         return remote(part, part, on_s.at[slot], on_r.at[slot], at_y(dy))
 
     def onward_in(dz):
         slot, dy = away.index(dz), (1 if dz % 2 == 0 else -1)
-        part = unit(dz, 2, lanes_b)
+        part = unit(dz, 2)
         return remote(part, part, on_s.at[slot], on_r.at[slot], at_y(dy))
 
     def route_a(stage):
@@ -220,45 +225,44 @@
         if stage == 1:
             for s in range(1, 4):
                 along_y_in(s).wait_recv()
-            right(0, 0).start()
-            left(0, 0).start()
-            to_sibling(0, lanes_a).start()
+            for s in (1, 7, 2, 6, 3, 5, 4):
+                groups_z(s).start()
+            to_sibling(0).start()
             return
         if stage > 5:
             return
-        right(1 - stage, stage - 2).wait_recv()
-        if stage < 5:
-            right(1 - stage, stage - 1).start()
-            left(stage - 1, stage - 2).wait_recv()
-            if stage < 4:
-                left(stage - 1, stage - 1).start()
-            to_sibling(1 - stage, lanes_a).start()
-            to_sibling(stage - 1, lanes_a).start()
-        else:
-            to_sibling(-4, lanes_a).start()
+        for dz in both(stage - 1):
+            groups_z_in(dz).wait_recv()
+            to_sibling(dz).start()
 
     def both(far):
         return (-4,) if far == 4 else (0,) if far == 0 else (-far, far)
 
     def route_b(stage):
+        arrive = {1: (-1, 1), 2: (-2, 2), 3: (-3, 3, -4)}
+        pass_on = {1: (0,), 3: (-1, 1), 4: (-2, 2), 5: (-3, 3, -4)}
+        take = {4: (0, -1, 1), 5: (-2, 2), 6: (-3, 3, -4)}
         if stage == 0:
-            for s in (1, 7, 2, 6, 3, 5, 4):
+            for s in (7, 1, 6, 2, 5, 3, 4):
                 along_z(s).start()
-        if stage <= 4:
-            for dz in both(stage):
-                if dz != 0:
-                    along_z_in(dz).wait_recv()
-                side(dz, 1).start()
-                side(dz, -1).start()
-        if 0 <= stage - 1 <= 4:
-            for dz in both(stage - 1):
-                side_in(dz, 1).wait_recv()
-                side_in(dz, -1).wait_recv()
-                onward(dz).start()
-        if 0 <= stage - 2 <= 4:
-            for dz in both(stage - 2):
-                onward_in(dz).wait_recv()
-                to_sibling(dz, lanes_b).start()
+            side(0, 1).start()
+            side(0, -1).start()
+            unit_to_sibling(0, 0).start()
+        for dz in arrive.get(stage, ()):
+            along_z_in(dz).wait_recv()
+            side(dz, 1).start()
+            side(dz, -1).start()
+            unit_to_sibling(dz, 0).start()
+        for dz in pass_on.get(stage, ()):
+            dy = 1 if dz % 2 == 0 else -1
+            side_in(dz, dy).wait_recv()
+            onward(dz).start()
+            unit_to_sibling(dz, -dy).start()
+            side_in(dz, -dy).wait_recv()
+            unit_to_sibling(dz, dy).start()
+        for dz in take.get(stage, ()):
+            onward_in(dz).wait_recv()
+            unit_to_sibling(dz, 2).start()
 
     def gather(stage):
         @pl.when(core == 0)
@@ -274,18 +278,18 @@
     own, other = tsend[...], trecv[...]
     @pl.when(core == 0)
     def _():
-        g_ref[y, z, :, lanes_a] = jnp.concatenate([own[:, 0:CUT], other[:, 0:CUT]], axis=0).astype(BF16)
+        ga[z, y, :, :] = jnp.concatenate([own[:, 0:CUT], other[:, 0:CUT]], axis=0).astype(BF16)
 
     @pl.when(core == 1)
     def _():
-        g_ref[y, z, :, lanes_b] = jnp.concatenate([other[:, CUT:KDIM], own[:, CUT:KDIM]], axis=0).astype(BF16)
+        gb[y, z, :, :] = jnp.concatenate([other[:, CUT:KDIM], own[:, CUT:KDIM]], axis=0).astype(BF16)
 
     gather(0)
     needs()
     for b in range(16):
         pltpu.make_async_copy(f_hbm.at[b], fv.at[b], fsem.at[b]).wait()
     done = 0
-    for stage, until in ((1, 2), (2, 5), (3, 8), (4, 11), (5, 14), (6, 16)):
+    for stage, until in ((1, 3), (2, 6), (3, 9), (4, 13), (5, 16)):
         integrals(done, until)
         done = until
         gather(stage)
@@ -300,91 +304,107 @@
             odd = d_ref[blocks[2 * m + 1], 2 * m + 1, :, 128:256]
             rhs[r, :, 1024 + m * 128:1024 + (m + 1) * 128] = jnp.where(lane256 < 64, even, odd)
 
-    @pl.when(core == 0)
-    def _():
-        for dz in away:
-            to_sibling(dz, lanes_b).wait_recv()
-
-    @pl.when(core == 1)
-    def _():
-        for dz in away:
-            to_sibling(dz, lanes_a).wait_recv()
-
-    def give(to, dx):
+    def from_sibling(part):
+        @pl.when(core == 0)
+        def _():
+            for dz in part:
+                for dy in range(4):
+                    unit_to_sibling(dz, dy).wait_recv()
+
+        @pl.when(core == 1)
+        def _():
+            for dz in part:
+                to_sibling(dz).wait_recv()
+
+    def give(h, to, dx):
         other = lax.rem(con + dx, 4)
         return remote(
-            xb.at[to, other], xr.at[y, dx], x_s.at[to, dx], x_r.at[y, dx], ((z * 4 + to) * 2 + core, other))
-
-    def given(src, dx):
-        return remote(xb.at[src, con], xr.at[src, dx], x_s.at[src, dx], x_r.at[src, dx], at_x(dx))
-
+            xb.at[h, to, other], xr.at[h, y, dx], x_s.at[h, to, dx], x_r.at[h, y, dx],
+            ((z * 4 + to) * 2 + core, other))
+
+    def given(h, src, dx):
+        return remote(
+            xb.at[h, src, con], xr.at[h, src, dx], x_s.at[h, src, dx], x_r.at[h, src, dx],
+            ((z * 4 + src) * 2 + core, lax.rem(con + dx, 4)))
+
+    parts = (away[0:4], away[4:8])
     for h in range(2):
-        rows = pl.ds(h * 256, 256)
-        left_side = g_ref[2 * h:2 * h + 2].reshape(256, KDIM)
+        if h == 1:
+            gather(6)
+        from_sibling(parts[h])
+        places = [lax.rem(z + dz + 8, 8) for dz in parts[h]]
+        left_side = jnp.concatenate(
+            [jnp.concatenate([ga[zz].reshape(64, CUT) for zz in places], axis=0),
+             jnp.concatenate([gb[:, zz, :, :].reshape(64, KDIM - CUT) for zz in places], axis=0)], axis=1)
+        need = jnp.concatenate([rneed[zz, :, :] for zz in places], axis=0)
         for r in range(NIRR):
             got = nt_dot(left_side, rhs[r])
             for k in range(2):
                 part = got[:, k * 128:(k + 1) * 128]
-                acc[k, rows, :] = part if r == 0 else jnp.where(rneed[rows, :] == float(r), part, acc[k, rows, :])
-        for j in range(2):
-            to = 2 * h + j
+                acc[k, :, :] = part if r == 0 else jnp.where(need == float(r), part, acc[k, :, :])
+        for to in range(4):
             for r in range(4):
                 for q in range(4):
                     for k in range(2):
-                        xf[pl.ds(r * 64 + q * 2 + k, 8, stride=8), :] = acc[
-                            k, pl.ds(to * 128 + (q // 2) * 8 + r * 2 + q % 2, 8, stride=16), :]
-            xb[to, :, :, :] = xf[...].astype(BF16).reshape(4, 64, 128)
+                        xf[pl.ds(r * 32 + q * 2 + k, 4, stride=8), :] = acc[
+                            k, pl.ds(to * 16 + (q // 2) * 8 + r * 2 + q % 2, 4, stride=64), :]
+            xb[h, to, :, :, :] = xf[...].astype(BF16).reshape(4, 32, 128)
             for dx in range(1, 4):
-                give(to, dx).start()
+                give(h, to, dx).start()
 
             @pl.when(y != to)
             def _():
-                give(to, 0).start()
-
-    xr[y, 0, :, :] = xb[y, con, :, :]
-    for src in range(4):
-        @pl.when(y != src)
-        def _():
-            given(src, 0).wait_recv()
-
-        for dx in range(1, 4):
-            given(src, dx).wait_recv()
-        total = (xr[src, 0].astype(F32) + xr[src, 1].astype(F32)) + (xr[src, 2].astype(F32) + xr[src, 3].astype(F32))
-        for zz in range(8):
-            for k in range(2):
-                zf[zz, k, src * 4:(src + 1) * 4, :] = total[zz * 8 + k * 4:zz * 8 + k * 4 + 4, :]
-    zb[...] = zf[...].astype(BF16)
-
-    def own_z(s, flip):
-        to = lax.rem(z + s, 8)
+                give(h, to, 0).start()
+
+        xr[h, y, 0, :, :] = xb[h, y, con, :, :]
+
+    def own_z(dz, flip):
+        to = lax.rem(z + dz + 8, 8)
         kk = 1 - core if flip else core
         return remote(
-            zb.at[to, kk], vb.at[core, z], ze_s.at[s, flip], ze_r.at[s, flip], ((to * 4 + y) * 2 + kk, con))
-
-    def own_z_in(s, flip):
-        src = lax.rem(z + 8 - s, 8)
+            zb.at[to, kk], vb.at[core, z], ze_s.at[dz % 8, flip], ze_r.at[dz % 8, flip],
+            ((to * 4 + y) * 2 + kk, con))
+
+    def own_z_in(dz, flip):
+        src = lax.rem(z + 8 - dz, 8)
         kk = 1 - core if flip else core
         return remote(
-            zb.at[src, kk], vb.at[kk, src], ze_s.at[s, flip], ze_r.at[s, flip], ((src * 4 + y) * 2 + kk, con))
-
-    routes = [(s, flip) for s in (4, 3, 5, 2, 6, 1, 7, 0) for flip in (0, 1) if (s, flip) != (0, 0)]
-    for s, flip in routes:
-        own_z(s, flip).start()
+            zb.at[src, kk], vb.at[kk, src], ze_s.at[dz % 8, flip], ze_r.at[dz % 8, flip],
+            ((src * 4 + y) * 2 + kk, con))
+
+    routes = [(dz, flip) for dz in away for flip in (0, 1) if (dz, flip) != (0, 0)]
+    for h in range(2):
+        places = [lax.rem(z + dz + 8, 8) for dz in parts[h]]
+        for src in range(4):
+            @pl.when(y != src)
+            def _():
+                given(h, src, 0).wait_recv()
+
+            for dx in range(1, 4):
+                given(h, src, dx).wait_recv()
+            total = (xr[h, src, 0].astype(F32) + xr[h, src, 1].astype(F32)) + (
+                xr[h, src, 2].astype(F32) + xr[h, src, 3].astype(F32))
+            for i in range(4):
+                for k in range(2):
+                    zf[i, k, src * 4:(src + 1) * 4, :] = total[i * 8 + k * 4:i * 8 + k * 4 + 4, :]
+        for i in range(4):
+            zb[places[i], :, :, :] = zf[i, :, :, :].astype(BF16)
+        for dz, flip in routes:
+            if dz in parts[h]:
+                own_z(dz, flip).start()
     vb[core, z, :, :] = zb[z, core, :, :]
-    for s, flip in routes:
-        own_z_in(s, flip).wait_recv()
+    for dz, flip in routes:
+        own_z_in(dz, flip).wait_recv()
     out_ref[...] = vb[...]
 
     @pl.when(core == 0)
     def _():
         for s in range(1, 4):
             along_y(s).wait_send()
-        for s in range(4):
-            right(-s, s).wait_send()
-        for s in range(3):
-            left(s, s).wait_send()
+        for s in range(1, 8):
+            groups_z(s).wait_send()
         for dz in away:
-            to_sibling(dz, lanes_a).wait_send()
+            to_sibling(dz).wait_send()
 
     @pl.when(core == 1)
     def _():
@@ -394,18 +414,20 @@
             side(dz, 1).wait_send()
             side(dz, -1).wait_send()
             onward(dz).wait_send()
-            to_sibling(dz, lanes_b).wait_send()
-
-    for to in range(4):
-        for dx in range(1, 4):
-            give(to, dx).wait_send()
-
-        @pl.when(y != to)
-        def _():
-            give(to, 0).wait_send()
-
-    for s, flip in routes:
-        own_z(s, flip).wait_send()
+            for dy in range(4):
+                unit_to_sibling(dz, dy).wait_send()
+
+    for h in range(2):
+        for to in range(4):
+            for dx in range(1, 4):
+                give(h, to, dx).wait_send()
+
+            @pl.when(y != to)
+            def _():
+                give(h, to, 0).wait_send()
+
+    for dz, flip in routes:
+        own_z(dz, flip).wait_send()
 
 
 def place_kernel(
@@ -488,21 +510,22 @@
             pltpu.VMEM((2, 64, 128), F32),
             pltpu.VMEM((8, KDIM), F32),
             pltpu.VMEM((8, KDIM), F32),
-            pltpu.VMEM((4, 8, 16, KDIM), BF16),
+            pltpu.VMEM((8, 4, 16, CUT), BF16),
+            pltpu.VMEM((4, 8, 16, KDIM - CUT), BF16),
             pltpu.VMEM((NIRR, 128, 256), BF16),
             pltpu.VMEM((NIRR, 8, 256, 256), BF16),
             pltpu.VMEM((NIRR, 256, KDIM), BF16),
-            pltpu.VMEM((512, 128), F32),
-            pltpu.VMEM((2, 512, 128), F32),
-            pltpu.VMEM((256, 128), F32),
-            pltpu.VMEM((4, 4, 64, 128), BF16),
-            pltpu.VMEM((4, 4, 64, 128), BF16),
-            pltpu.VMEM((8, 2, 16, 128), F32),
+            pltpu.VMEM((8, 64, 128), F32),
+            pltpu.VMEM((2, 256, 128), F32),
+            pltpu.VMEM((128, 128), F32),
+            pltpu.VMEM((2, 4, 4, 32, 128), BF16),
+            pltpu.VMEM((2, 4, 4, 32, 128), BF16),
+            pltpu.VMEM((4, 2, 16, 128), F32),
             pltpu.VMEM((8, 2, 16, 128), BF16),
             pltpu.VMEM((2, 8, 16, 128), BF16),
-            dma((16,)), dma, dma, dma((3,)), dma((3,)), dma((4,)), dma((4,)), dma((3,)), dma((3,)),
-            dma((8,)), dma((8,)), dma((7,)), dma((7,)), dma((8, 2)), dma((8, 2)), dma((8,)), dma((8,)),
-            dma((4, 4)), dma((4, 4)), dma((8, 2)), dma((8, 2)),
+            dma((16,)), dma, dma, dma((3,)), dma((3,)), dma((7,)), dma((7,)),
+            dma((8,)), dma((8,)), dma((8, 4)), dma((8, 4)), dma((7,)), dma((7,)), dma((8, 2)), dma((8, 2)), dma((8,)), dma((8,)),
+            dma((2, 4, 4)), dma((2, 4, 4)), dma((8, 2)), dma((8, 2)),
         ],
         compiler_params=pltpu.CompilerParams(
             collective_id=0, has_side_effects=True, vmem_limit_bytes=48 * 1024 * 1024),

time: 49.5 us -> 47.6 us (0.962)
  Pallas kernels: 47.5 us -> 45.6 us
    pallas_call x1, Pallas kernels: 45.3 us -> 43.4 us  [ladder(): pl.pallas_call(ladder_kernel, out_shape=jax.ShapeDtypeStruct((2, 8, 16, 1...]
where the time goes in v3:
time: 47.6 us; the launch traced here: 47.5 us
  Pallas kernels  45.6 us (96%)
  local copies, waits for them, and re-layouts  0.87 us (2%)
  loops' own time  0.82 us (2%)
    pallas_call x1, Pallas kernels, ladder(): pl.pallas_call(ladder_kernel, out_shape=jax.ShapeDtypeStruct((2, 8, 16, 1...  43.4 us
    pallas_call x1, Pallas kernels, place(): pl.pallas_call(functools.partial(place_kernel, first_round=first_round),...  2.26 us

profile of v3, /device:TPU:1, one launch (start us, length us, event | category | flops | bytes accessed | tf_op | source)
XLA Modules:
  0.0 47.5 jit_solution(2568319880995446515)
XLA Ops:
  0.0 0.0 copy-start.1
  0.0 0.0 copy-start.3
  0.0 0.0 copy-start.2
  0.0 0.0 copy-start.5
  0.0 0.0 copy-start.8
  0.0 0.0 copy-start.9
  0.0 0.0 copy-start.4
  0.0 0.0 copy-start.6
  0.1 0.0 copy-start.7
  0.1 43.4 %ladder.2.v_ref = bf16[2,8,16,128]{3,2,1,0:T(8,128)(2,1)S(1)} custom-call(s32[512]{0:T(512)} %pair_s.3, s32[64]{0:T(128)} %airr_s.1, s32[8]{0:T(128)} %cirr_s.1, s32[8]{0:T(128)} %start_s.1, s32[8,8]{1,0:T(8,128)} %prod_s.3, s32[64]{0:T(128)} %tirr_s.1, s32[1]{0:T(128)} %constant.2.clone.1.round_s, bf16[8,8,800]{2,1,0:T(8,128)(2,1)} %amp_ref.1, ...), custom_call_target="tpu_custom_call" | custom-call | tf_op jit(solution)/shard_map/ladder/pallas_call | solution.py:502
  43.5 0.0 copy-done.3
  43.5 0.0 copy-done.5
  43.5 0.0 copy-done.4
  43.5 0.0 copy-done.6
  43.5 0.0 copy-done.7
  43.5 2.3 %place_more.2 = (f32[2,64,1024]{2,1,0:T(8,128)S(1)}, s32[1]{0:T(128)}) custom-call(s32[512]{0:T(512)S(1)} %copy-done.3, s32[8,8]{1,0:T(8,128)S(1)} %copy-done.4, s32[1]{0:T(128)} %constant.2.clone.1.round_s, s32[1,64]{1,0:T(1,128)S(1)} %bitcast.24, s32[1,64]{1,0:T(1,128)S(1)} %bitcast.32, s32[1,64]{1,0:T(1,128)S(1)} %bitcast.28, ...), custom_call_target="tpu_custom_call" | custom-call | tf_op jit(solution)/shard_map/place_more/pallas_call | solution.py:537
  45.8 0.0 copy-done.1
  45.8 0.0 copy-done.2
  45.8 0.0 copy-done.8
  45.8 0.0 copy-done.9
  45.8 0.8 %while.10 = (s32[]{:T(128)}, f32[2,64,1024]{2,1,0:T(8,128)S(1)}, s32[1]{0:T(128)}, s32[512]{0:T(512)S(1)}, s32[64]{0:T(128)S(1)}, /*index=5*/s32[8]{0:T(128)S(1)...) while((s32[]{:T(128)}, f32[2,64,1024]{2,1,0:T(8,128)S(1)}, ...), condition=%wide.region_1.0_spmd, body=%wide.region_0.0_spmd.sunk | while | flops 2 | bytes 1048733 | solution.py:570
  46.7 0.0 copy-start
  46.7 0.8 %copy-done = f32[2,64,1024]{2,1,0:T(8,128)} copy-done((f32[2,64,1024]{2,1,0:T(8,128)}, f32[2,64,1024]{2,1,0:T(8,128)S(1)}, u32[]{:S(2)}) %copy-start) | copy-done | bytes 524312
  (1 shorter events, 0.0 us)
Async XLA Ops:
  0.0 45.8 %copy-start.1 = (bf16[256,64,8]{0,2,1:T(8,128)(2,1)S(1)}, bf16[256,64,8]{0,2,1:T(8,128)(2,1)}, u32[]{:S(2)}) copy-start(bf16[256,64,8]{0,2,1:T(8,128)(2,1)} %param.14) | copy-start | bytes 786436
  0.0 43.5 %copy-start.3 = (s32[512]{0:T(512)S(1)}, s32[512]{0:T(512)}, u32[]{:S(2)}) copy-start(s32[512]{0:T(512)} %pair_s.3) | copy-start | bytes 6148
  0.0 45.8 %copy-start.2 = (bf16[8,8,800]{2,1,0:T(8,128)(2,1)S(1)}, bf16[8,8,800]{2,1,0:T(8,128)(2,1)}, u32[]{:S(2)}) copy-start(bf16[8,8,800]{2,1,0:T(8,128)(2,1)} %amp_ref.1) | copy-start | bytes 307204
  0.0 43.5 %copy-start.5 = (s32[64]{0:T(128)S(1)}, s32[64]{0:T(128)}, u32[]{:S(2)}) copy-start(s32[64]{0:T(128)} %airr_s.1) | copy-start | bytes 772
  0.0 45.8 %copy-start.8 = (s32[8]{0:T(128)S(1)}, s32[8]{0:T(128)}, u32[]{:S(2)}) copy-start(s32[8]{0:T(128)} %cirr_s.1) | copy-start | bytes 100
  0.0 45.8 %copy-start.9 = (s32[8]{0:T(128)S(1)}, s32[8]{0:T(128)}, u32[]{:S(2)}) copy-start(s32[8]{0:T(128)} %start_s.1) | copy-start | bytes 100
  0.0 43.5 %copy-start.4 = (s32[8,8]{1,0:T(8,128)S(1)}, s32[8,8]{1,0:T(8,128)}, u32[]{:S(2)}) copy-start(s32[8,8]{1,0:T(8,128)} %prod_s.3) | copy-start | bytes 772
  0.0 43.5 %copy-start.6 = (s32[64]{0:T(128)S(1)}, s32[64]{0:T(128)}, u32[]{:S(2)}) copy-start(s32[64]{0:T(128)} %tirr_s.1) | copy-start | bytes 772
  0.1 43.5 %copy-start.7 = (s32[64]{0:T(128)S(1)}, s32[64]{0:T(128)}, u32[]{:S(2)}) copy-start(s32[64]{0:T(128)} %param.20) | copy-start | bytes 772
  46.7 0.8 %copy-start = (f32[2,64,1024]{2,1,0:T(8,128)}, f32[2,64,1024]{2,1,0:T(8,128)S(1)}, u32[]{:S(2)}) copy-start(f32[2,64,1024]{2,1,0:T(8,128)S(1)} %get-tuple-element.277) | copy-start | bytes 1572868

commit v4 on v3

--- a/solution.py
+++ b/solution.py
@@ -148,15 +148,12 @@
             rneed[2 * k + 1, :, :] = column[64:128, :]
 
     def integrals(begin, end):
-        def one(b, carry):
+        for b in range(begin, end):
             for g in range(NIRR):
                 main = fv[b, pl.ds(first[g], 6), :, :].reshape(WIN, 256)
                 tail = fv[b, pl.ds(first[g] + 4, 2), :, :].reshape(64, 256)
                 got = nt_dot(asel[g], jnp.concatenate([main, tail], axis=0))
-                d_ref[g, :, pl.ds(pl.multiple_of(b * 16, 16), 16), :] = got.astype(BF16).reshape(8, 16, 256)
-            return carry
-
-        lax.fori_loop(begin, end, one, 0)
+                d_ref[g, :, b * 16:(b + 1) * 16, :] = got.astype(BF16).reshape(8, 16, 256)
 
     def unit_a(dy):
         return ga.at[z, lax.rem(y + dy + 4, 4)]
@@ -289,7 +286,7 @@
     for b in range(16):
         pltpu.make_async_copy(f_hbm.at[b], fv.at[b], fsem.at[b]).wait()
     done = 0
-    for stage, until in ((1, 3), (2, 6), (3, 9), (4, 13), (5, 16)):
+    for stage, until in ((1, 4), (2, 8), (3, 11), (4, 14), (5, 16)):
         integrals(done, until)
         done = until
         gather(stage)
@@ -329,8 +326,6 @@
 
     parts = (away[0:4], away[4:8])
     for h in range(2):
-        if h == 1:
-            gather(6)
         from_sibling(parts[h])
         places = [lax.rem(z + dz + 8, 8) for dz in parts[h]]
         left_side = jnp.concatenate(
@@ -338,6 +333,8 @@
              jnp.concatenate([gb[:, zz, :, :].reshape(64, KDIM - CUT) for zz in places], axis=0)], axis=1)
         need = jnp.concatenate([rneed[zz, :, :] for zz in places], axis=0)
         for r in range(NIRR):
+            if h == 0 and r == 6:
+                gather(6)
             got = nt_dot(left_side, rhs[r])
             for k in range(2):
                 part = got[:, k * 128:(k + 1) * 128]

time: 47.6 us -> 46.4 us (0.975)
  Pallas kernels: 45.6 us -> 44.6 us
    pallas_call x1, Pallas kernels: 43.4 us -> 42.3 us  [ladder(): pl.pallas_call(ladder_kernel, out_shape=jax.ShapeDtypeStruct((2, 8, 16, 1...]
where the time goes in v4:
time: 46.4 us; the launch traced here: 46.3 us
  Pallas kernels  44.6 us (96%)
  local copies, waits for them, and re-layouts  0.87 us (2%)
  loops' own time  0.64 us (1%)
    pallas_call x1, Pallas kernels, ladder(): pl.pallas_call(ladder_kernel, out_shape=jax.ShapeDtypeStruct((2, 8, 16, 1...  42.3 us
    pallas_call x1, Pallas kernels, place(): pl.pallas_call(functools.partial(place_kernel, first_round=first_round),...  2.27 us

profile of v4, /device:TPU:1, one launch (start us, length us, event | category | flops | bytes accessed | tf_op | source)
XLA Modules:
  0.0 46.3 jit_solution(9474392891785891719)
XLA Ops:
  0.0 0.0 copy-start.1
  0.0 0.0 copy-start.3
  0.0 0.0 copy-start.2
  0.0 0.0 copy-start.5
  0.0 0.0 copy-start.8
  0.0 0.0 copy-start.9
  0.0 0.0 copy-start.4
  0.0 0.0 copy-start.6
  0.1 0.0 copy-start.7
  0.1 42.3 %ladder.2.v_ref = bf16[2,8,16,128]{3,2,1,0:T(8,128)(2,1)S(1)} custom-call(s32[512]{0:T(512)} %pair_s.3, s32[64]{0:T(128)} %airr_s.1, s32[8]{0:T(128)} %cirr_s.1, s32[8]{0:T(128)} %start_s.1, s32[8,8]{1,0:T(8,128)} %prod_s.3, s32[64]{0:T(128)} %tirr_s.1, s32[1]{0:T(128)} %constant.2.clone.1.round_s, bf16[8,8,800]{2,1,0:T(8,128)(2,1)} %amp_ref.1, ...), custom_call_target="tpu_custom_call" | custom-call | tf_op jit(solution)/shard_map/ladder/pallas_call | solution.py:499
  42.4 0.0 copy-done.3
  42.4 0.0 copy-done.5
  42.5 0.0 copy-done.4
  42.5 0.0 copy-done.6
  42.5 0.0 copy-done.7
  42.5 2.3 %place_more.2 = (f32[2,64,1024]{2,1,0:T(8,128)S(1)}, s32[1]{0:T(128)}) custom-call(s32[512]{0:T(512)S(1)} %copy-done.3, s32[8,8]{1,0:T(8,128)S(1)} %copy-done.4, s32[1]{0:T(128)} %constant.2.clone.1.round_s, s32[1,64]{1,0:T(1,128)S(1)} %bitcast.24, s32[1,64]{1,0:T(1,128)S(1)} %bitcast.32, s32[1,64]{1,0:T(1,128)S(1)} %bitcast.28, ...), custom_call_target="tpu_custom_call" | custom-call | tf_op jit(solution)/shard_map/place_more/pallas_call | solution.py:534
  44.8 0.0 copy-done.1
  44.8 0.0 copy-done.2
  44.8 0.0 copy-done.8
  44.8 0.0 copy-done.9
  44.8 0.6 %while.10 = (s32[]{:T(128)}, f32[2,64,1024]{2,1,0:T(8,128)S(1)}, s32[1]{0:T(128)}, s32[512]{0:T(512)S(1)}, s32[64]{0:T(128)S(1)}, /*index=5*/s32[8]{0:T(128)S(1)...) while((s32[]{:T(128)}, f32[2,64,1024]{2,1,0:T(8,128)S(1)}, ...), condition=%wide.region_1.0_spmd, body=%wide.region_0.0_spmd.sunk | while | flops 2 | bytes 1048733 | solution.py:567
  45.5 0.0 copy-start
  45.5 0.8 %copy-done = f32[2,64,1024]{2,1,0:T(8,128)} copy-done((f32[2,64,1024]{2,1,0:T(8,128)}, f32[2,64,1024]{2,1,0:T(8,128)S(1)}, u32[]{:S(2)}) %copy-start) | copy-done | bytes 524312
  (1 shorter events, 0.0 us)
Async XLA Ops:
  0.0 44.8 %copy-start.1 = (bf16[256,64,8]{0,2,1:T(8,128)(2,1)S(1)}, bf16[256,64,8]{0,2,1:T(8,128)(2,1)}, u32[]{:S(2)}) copy-start(bf16[256,64,8]{0,2,1:T(8,128)(2,1)} %param.14) | copy-start | bytes 786436
  0.0 42.4 %copy-start.3 = (s32[512]{0:T(512)S(1)}, s32[512]{0:T(512)}, u32[]{:S(2)}) copy-start(s32[512]{0:T(512)} %pair_s.3) | copy-start | bytes 6148
  0.0 44.8 %copy-start.2 = (bf16[8,8,800]{2,1,0:T(8,128)(2,1)S(1)}, bf16[8,8,800]{2,1,0:T(8,128)(2,1)}, u32[]{:S(2)}) copy-start(bf16[8,8,800]{2,1,0:T(8,128)(2,1)} %amp_ref.1) | copy-start | bytes 307204
  0.0 42.4 %copy-start.5 = (s32[64]{0:T(128)S(1)}, s32[64]{0:T(128)}, u32[]{:S(2)}) copy-start(s32[64]{0:T(128)} %airr_s.1) | copy-start | bytes 772
  0.0 44.8 %copy-start.8 = (s32[8]{0:T(128)S(1)}, s32[8]{0:T(128)}, u32[]{:S(2)}) copy-start(s32[8]{0:T(128)} %cirr_s.1) | copy-start | bytes 100
  0.0 44.8 %copy-start.9 = (s32[8]{0:T(128)S(1)}, s32[8]{0:T(128)}, u32[]{:S(2)}) copy-start(s32[8]{0:T(128)} %start_s.1) | copy-start | bytes 100
  0.0 42.4 %copy-start.4 = (s32[8,8]{1,0:T(8,128)S(1)}, s32[8,8]{1,0:T(8,128)}, u32[]{:S(2)}) copy-start(s32[8,8]{1,0:T(8,128)} %prod_s.3) | copy-start | bytes 772
  0.0 42.4 %copy-start.6 = (s32[64]{0:T(128)S(1)}, s32[64]{0:T(128)}, u32[]{:S(2)}) copy-start(s32[64]{0:T(128)} %tirr_s.1) | copy-start | bytes 772
  0.1 42.4 %copy-start.7 = (s32[64]{0:T(128)S(1)}, s32[64]{0:T(128)}, u32[]{:S(2)}) copy-start(s32[64]{0:T(128)} %param.20) | copy-start | bytes 772
  45.5 0.8 %copy-start = (f32[2,64,1024]{2,1,0:T(8,128)}, f32[2,64,1024]{2,1,0:T(8,128)S(1)}, u32[]{:S(2)}) copy-start(f32[2,64,1024]{2,1,0:T(8,128)S(1)} %get-tuple-element.277) | copy-start | bytes 1572868
